TPU v7x, 32 devices: a whole 2x2x4 slice. The times are simulated.
32 devices in a mesh: dp: 8 (over y, x, core), mp: 4 (over z).
Axes of the slice: x: 2, y: 2, z: 4, core: 2. Of those that a mesh axis runs over, the one named last changes fastest.
Arguments:
- tokens: bfloat16 [16384, 768], P(('dp', 'mp')), may hold values from -6 to 6
- region_mask: int32 [128, 128], P('dp'), may hold values from 0 to 1, as said below
- attn_gain: bfloat16 [768], replicated, may hold values from 0.25 to 1.75
- self_qkv: bfloat16 [3, 768, 768], P(None, 'mp'), may hold values from -0.21875 to 0.21875
- cross_qkv: bfloat16 [3, 768, 768], P(None, 'mp'), may hold values from -0.21875 to 0.21875
- self_out: bfloat16 [768, 768], P('mp'), may hold values from -1.25 to 1.25
- cross_out: bfloat16 [768, 768], P('mp'), may hold values from -1.25 to 1.25
- gate_weight: bfloat16 [768, 768], replicated, may hold values from -0.21875 to 0.21875
- gate_bias: bfloat16 [768], replicated, may hold values from -4 to 4
- ffn_gain: bfloat16 [768], replicated, may hold values from 0.25 to 1.75
- up_weight: bfloat16 [768, 3072], P(None, 'mp'), may hold values from -0.21875 to 0.21875
- down_weight: bfloat16 [3072, 768], P('mp'), may hold values from -0.109375 to 0.109375
- out_grad: bfloat16 [16384, 768], P(('dp', 'mp')), may hold values from -6 to 6
Outputs:
- out: bfloat16 [16384, 768], P(('dp', 'mp'))
- tokens_grad: bfloat16 [16384, 768], P(('dp', 'mp'))
- attn_gain_grad: float32 [768], replicated
- self_qkv_grad: float32 [3, 768, 768], P(None, 'mp')
- cross_qkv_grad: float32 [3, 768, 768], P(None, 'mp')
- self_out_grad: float32 [768, 768], P('mp')
- cross_out_grad: float32 [768, 768], P('mp')
- gate_weight_grad: float32 [768, 768], replicated
- gate_bias_grad: float32 [768], replicated
- ffn_gain_grad: float32 [768], replicated
- up_weight_grad: float32 [768, 3072], P(None, 'mp')
- down_weight_grad: float32 [3072, 768], P('mp')
Inputs may be any that keep to these rules, and one draw needn't show every extreme that they name: `region_mask`: in each page the real language regions fill the first of the 96 language slots and the real vision regions the first of the 32 vision slots; every page has one or more of each, and some page has all 128 slots real.
All inputs are finite; a program needn't handle non-finite values.
Results may differ from a plain program's by a relative error of at most 0.012.
The roundings to bfloat16 on the way count: a program that leaves them out, or rounds other values in their place, can miss the bound.
Values may be sent and summed in bfloat16 or wider, within the bound.
A program may use at most 192 MiB of HBM per device.

v0:
```python
import functools

import jax
import jax.numpy as jnp
from jax import lax
from jax.sharding import PartitionSpec as P

HEAD_DIM = 64
LANG = 96
SLOTS = 128


epsilon = 1e-05
neg_fill = -1e30


def standardize(full_rows):
    centre = jnp.mean(full_rows, axis=1, keepdims=True)
    offset = full_rows - centre
    spread = jnp.mean(offset * offset, axis=1, keepdims=True)
    inv_std = lax.rsqrt(spread + epsilon)
    return (offset * inv_std, inv_std)


def own_rows(full_rows, row_start, row_count):
    return lax.dynamic_slice_in_dim(full_rows, row_start, row_count, 0)


def attend_forward(normed, weight, allowed, page_count):
    col_count = weight.shape[1]
    heads_here = col_count // HEAD_DIM
    triple = jnp.einsum("td,cfd->tcf", normed, weight, preferred_element_type=jnp.float32)
    triple = triple.astype(jnp.bfloat16).reshape(page_count, SLOTS, 3, heads_here, HEAD_DIM)
    scores = jnp.einsum(
        "pqhe,pkhe->phqk", triple[:, :, 0], triple[:, :, 1], preferred_element_type=jnp.float32
    ) * HEAD_DIM ** (-0.5)
    scores = jnp.where(allowed[:, None], scores, neg_fill)
    log_total = jax.nn.logsumexp(scores, axis=-1, keepdims=True)
    attention = jnp.exp(scores - log_total).astype(jnp.bfloat16)
    mixture = jnp.einsum(
        "phqk,pkhe->pqhe", attention, triple[:, :, 2], preferred_element_type=jnp.float32
    )
    mixture = mixture.astype(jnp.bfloat16).reshape(page_count * SLOTS, col_count)
    return (mixture, (triple, log_total))


def attend_backward(grad_mixture, saved, allowed, page_count):
    triple, log_total = saved
    queries = triple[:, :, 0]
    keys_part = triple[:, :, 1]
    values_part = triple[:, :, 2]
    heads_here = triple.shape[3]
    scores = jnp.einsum(
        "pqhe,pkhe->phqk", queries, keys_part, preferred_element_type=jnp.float32
    ) * HEAD_DIM ** (-0.5)
    scores = jnp.where(allowed[:, None], scores, neg_fill)
    attention = jnp.exp(scores - log_total)
    grad_mix = grad_mixture.reshape(page_count, SLOTS, heads_here, HEAD_DIM)
    grad_values = jnp.einsum(
        "phqk,pqhe->pkhe",
        attention.astype(jnp.bfloat16),
        grad_mix,
        preferred_element_type=jnp.float32,
    )
    grad_attention = jnp.einsum(
        "pqhe,pkhe->phqk", grad_mix, values_part, preferred_element_type=jnp.float32
    )
    grad_scores = attention * (
        grad_attention - jnp.sum(attention * grad_attention, axis=-1, keepdims=True)
    )
    grad_scores = grad_scores.astype(jnp.bfloat16)
    grad_queries = jnp.einsum(
        "phqk,pkhe->pqhe", grad_scores, keys_part, preferred_element_type=jnp.float32
    ) * HEAD_DIM ** (-0.5)
    grad_keys = jnp.einsum(
        "phqk,pqhe->pkhe", grad_scores, queries, preferred_element_type=jnp.float32
    ) * HEAD_DIM ** (-0.5)
    stacked = jnp.stack([grad_queries, grad_keys, grad_values], axis=2).astype(jnp.bfloat16)
    return stacked.reshape(page_count * SLOTS, 3, heads_here * HEAD_DIM)


def norm_backward(grad_normed, unit_rows, inv_std, gain):
    scaled = grad_normed * gain
    first = jnp.mean(scaled, axis=1, keepdims=True)
    second = jnp.mean(scaled * unit_rows, axis=1, keepdims=True)
    return (
        inv_std * (scaled - first - unit_rows * second),
        jnp.sum(grad_normed * unit_rows, axis=0),
    )


def body(
    tokens,
    region_mask,
    attn_gain,
    self_qkv,
    cross_qkv,
    self_out,
    cross_out,
    gate_weight,
    gate_bias,
    ffn_gain,
    up_weight,
    down_weight,
    out_grad,
):
    page_count = region_mask.shape[0]
    rows_here = tokens.shape[0]
    row_start = lax.axis_index("mp") * rows_here
    modality = jnp.arange(SLOTS) >= LANG
    same_kind = modality[:, None] == modality[None, :]
    real_key = region_mask[:, None, :] > 0
    allow_self = same_kind[None] & real_key
    allow_cross = jnp.logical_not(same_kind)[None] & real_key
    gain_one = attn_gain.astype(jnp.float32)
    gain_two = ffn_gain.astype(jnp.float32)
    resid_in = tokens.astype(jnp.float32)
    unit_one, inv_one = standardize(resid_in)
    normed_own = (unit_one * gain_one).astype(jnp.bfloat16)
    normed = lax.all_gather(normed_own, "mp", axis=0, tiled=True)
    self_mix, self_saved = attend_forward(normed, self_qkv, allow_self, page_count)
    cross_mix, cross_saved = attend_forward(normed, cross_qkv, allow_cross, page_count)
    self_part = jnp.dot(self_mix, self_out, preferred_element_type=jnp.float32)
    cross_part = jnp.dot(cross_mix, cross_out, preferred_element_type=jnp.float32)
    self_branch, cross_branch = (
        lax.psum_scatter(self_part, "mp", scatter_dimension=0, tiled=True),
        lax.psum_scatter(cross_part, "mp", scatter_dimension=0, tiled=True),
    )
    gate_pre = jnp.dot(
        normed_own, gate_weight, preferred_element_type=jnp.float32
    ) + gate_bias.astype(jnp.float32)
    gate_open = jax.nn.sigmoid(gate_pre)
    middle = resid_in + gate_open * self_branch + (1.0 - gate_open) * cross_branch
    full_mid = lax.all_gather(middle, "mp", axis=0, tiled=True)
    unit_mid, inv_mid = standardize(full_mid)
    normed_two = (unit_mid * gain_two).astype(jnp.bfloat16)
    unit_two = own_rows(unit_mid, row_start, rows_here)
    inv_two = own_rows(inv_mid, row_start, rows_here)
    inner_act = jnp.dot(normed_two, up_weight, preferred_element_type=jnp.float32)
    activated, gelu_pull = jax.vjp(functools.partial(jax.nn.gelu, approximate=True), inner_act)
    hidden = activated.astype(jnp.bfloat16)
    ffn_part = jnp.dot(hidden, down_weight, preferred_element_type=jnp.float32)
    ffn_rows = lax.psum_scatter(
        ffn_part.astype(jnp.bfloat16), "mp", scatter_dimension=0, tiled=True
    ).astype(jnp.float32)
    result = (middle + ffn_rows).astype(jnp.bfloat16)
    grad_full = lax.all_gather(out_grad, "mp", axis=0, tiled=True)
    grad_down = jnp.einsum("tf,td->fd", hidden, grad_full, preferred_element_type=jnp.float32)
    grad_hidden = jnp.einsum(
        "td,fd->tf", grad_full, down_weight, preferred_element_type=jnp.float32
    )
    grad_inner = gelu_pull(grad_hidden)[0].astype(jnp.bfloat16)
    grad_up = jnp.einsum("td,tf->df", normed_two, grad_inner, preferred_element_type=jnp.float32)
    grad_normed_two_part = jnp.einsum(
        "tf,df->td", grad_inner, up_weight, preferred_element_type=jnp.float32
    )
    grad_normed_two = lax.psum_scatter(grad_normed_two_part, "mp", scatter_dimension=0, tiled=True)
    back_two, grad_gain_two = norm_backward(grad_normed_two, unit_two, inv_two, gain_two)
    grad_middle = out_grad.astype(jnp.float32) + back_two
    grad_self = (gate_open * grad_middle).astype(jnp.bfloat16)
    grad_cross = ((1.0 - gate_open) * grad_middle).astype(jnp.bfloat16)
    grad_gate_pre = (
        grad_middle * (self_branch - cross_branch) * gate_open * (1.0 - gate_open)
    ).astype(jnp.bfloat16)
    grad_gate_weight = jnp.einsum(
        "td,tc->dc", normed_own, grad_gate_pre, preferred_element_type=jnp.float32
    )
    grad_gate_bias = jnp.sum(grad_gate_pre.astype(jnp.float32), axis=0)
    full_self, full_cross = (
        lax.all_gather(grad_self, "mp", axis=0, tiled=True),
        lax.all_gather(grad_cross, "mp", axis=0, tiled=True),
    )
    grad_self_out = jnp.einsum("tc,td->cd", self_mix, full_self, preferred_element_type=jnp.float32)
    grad_cross_out = jnp.einsum(
        "tc,td->cd", cross_mix, full_cross, preferred_element_type=jnp.float32
    )
    grad_self_mix = jnp.einsum(
        "td,cd->tc", full_self, self_out, preferred_element_type=jnp.float32
    ).astype(jnp.bfloat16)
    grad_cross_mix = jnp.einsum(
        "td,cd->tc", full_cross, cross_out, preferred_element_type=jnp.float32
    ).astype(jnp.bfloat16)
    self_stack = attend_backward(grad_self_mix, self_saved, allow_self, page_count)
    cross_stack = attend_backward(grad_cross_mix, cross_saved, allow_cross, page_count)
    grad_self_qkv = jnp.einsum(
        "tcf,td->cfd", self_stack, normed, preferred_element_type=jnp.float32
    )
    grad_cross_qkv = jnp.einsum(
        "tcf,td->cfd", cross_stack, normed, preferred_element_type=jnp.float32
    )
    grad_normed_part = jnp.einsum(
        "tcf,cfd->td", self_stack, self_qkv, preferred_element_type=jnp.float32
    )
    grad_normed_part = grad_normed_part + jnp.einsum(
        "tcf,cfd->td", cross_stack, cross_qkv, preferred_element_type=jnp.float32
    )
    grad_normed = lax.psum_scatter(grad_normed_part, "mp", scatter_dimension=0, tiled=True)
    grad_normed = grad_normed + jnp.einsum(
        "tc,dc->td", grad_gate_pre, gate_weight, preferred_element_type=jnp.float32
    )
    back_one, grad_gain_one = norm_backward(grad_normed, unit_one, inv_one, gain_one)
    grad_tokens = (grad_middle + back_one).astype(jnp.bfloat16)
    summed = lax.psum(
        (grad_self_qkv, grad_cross_qkv, grad_self_out, grad_cross_out, grad_up, grad_down), "dp"
    )
    shared = lax.psum(
        (grad_gain_one, grad_gate_weight, grad_gate_bias, grad_gain_two), ("dp", "mp")
    )
    return (
        result,
        grad_tokens,
        shared[0],
        summed[0],
        summed[1],
        summed[2],
        summed[3],
        shared[1],
        shared[2],
        shared[3],
        summed[4],
        summed[5],
    )


def solution(mesh):
    placed = (
        P(("dp", "mp"), None),
        P("dp", None),
        P(),
        P(None, "mp", None),
        P(None, "mp", None),
        P("mp", None),
        P("mp", None),
        P(),
        P(),
        P(),
        P(None, "mp"),
        P("mp", None),
        P(("dp", "mp"), None),
    )
    return jax.shard_map(
        body,
        mesh=mesh,
        in_specs=placed,
        out_specs=(
            P(("dp", "mp"), None),
            P(("dp", "mp"), None),
            P(),
            P(None, "mp", None),
            P(None, "mp", None),
            P("mp", None),
            P("mp", None),
            P(),
            P(),
            P(),
            P(None, "mp"),
            P("mp", None),
        ),
        check_vma=False,
    )
```

profile of v0, /device:TPU:0, one launch (start us, length us, event | category | flops | bytes accessed | tf_op | source)
XLA Modules:
  0.0 1246.1 jit_solution(1636475710774246501)
XLA Ops:
  7.3 1.4 convert_reduce_fusion
  8.7 1.5 fusion.38
  10.9 2.3 fusion.31
  14.0 65.7 %all-gather.6.cloned.1.call-done = bf16[2048,768]{1,0:T(8,128)(2,1)} async-done(((bf16[512,768]{1,0:T(8,128)(2,1)}), bf16[2048,768]{1,0:T(8,128)(2,1)}) %all-gather.6.cloned.1.call-update) | async-done | bytes 3145744 | tf_op jit(solution)/shard_map/all_gather | solution.py:120
  79.6 3.9 fusion.18
  89.9 3.7 fusion.54
  94.7 3.9 fusion.15
  105.0 3.7 fusion.58
  109.4 93.8 %reduce-scatter.8.cloned.1.call-done = f32[512,768]{1,0:T(8,128)} async-done(((f32[2048,768]{1,0:T(8,128)}), f32[512,768]{1,0:T(8,128)}) %reduce-scatter.8.cloned.1.call-update) | async-done | bytes 1572880 | tf_op jit(solution)/shard_map/reduce_scatter | solution.py:127
  203.1 113.6 %reduce-scatter.6.cloned.1.call-done = f32[512,768]{1,0:T(8,128)} async-done(((f32[2048,768]{1,0:T(8,128)}), f32[512,768]{1,0:T(8,128)}) %reduce-scatter.6.cloned.1.call-update) | async-done | bytes 1572880 | tf_op jit(solution)/shard_map/reduce_scatter | solution.py:126
  316.8 5.2 fusion.39
  322.3 60.0 %all-gather.10.cloned.1.call-done = bf16[2048,768]{1,0:T(8,128)(2,1)} async-done(((bf16[512,768]{1,0:T(8,128)(2,1)}), bf16[2048,768]{1,0:T(8,128)(2,1)}) %all-gather.10.cloned.1.call-update) | async-done | bytes 3145744 | tf_op jit(solution)/shard_map/all_gather | solution.py:147
  382.2 7.2 fusion.83
  389.4 108.3 %all-gather.8.cloned.1.call-done = f32[2048,768]{1,0:T(8,128)} async-done(((f32[512,768]{1,0:T(8,128)}), f32[2048,768]{1,0:T(8,128)}) %all-gather.8.cloned.1.call-update) | async-done | bytes 6291472 | tf_op jit(solution)/shard_map/all_gather | solution.py:134
  497.7 3.1 reduce_sum.139
  500.9 3.7 multiply_reduce_fusion
  507.6 7.5 fusion.6
  515.0 1.7 copy-done.35
  516.7 4.5 fusion.84
  521.4 109.0 %reduce-scatter.12.cloned.1.call-done = f32[512,768]{1,0:T(8,128)} async-done(((f32[2048,768]{1,0:T(8,128)}), f32[512,768]{1,0:T(8,128)}) %reduce-scatter.12.cloned.1.call-update) | async-done | bytes 1572880 | tf_op jit(solution)/shard_map/reduce_scatter | solution.py:157
  630.4 2.4 multiply_reduce_fusion.3
  632.9 4.7 convert_reduce_fusion.1
  637.6 1.5 multiply_convert_fusion.7
  640.4 8.6 convolution_convert_fusion
  649.0 54.2 %all-gather.14.cloned.1.call-done = bf16[2048,768]{1,0:T(8,128)(2,1)} async-done(((bf16[512,768]{1,0:T(8,128)(2,1)}), bf16[2048,768]{1,0:T(8,128)(2,1)}) %all-gather.14.cloned.1.call-update) | async-done | bytes 3145744 | tf_op jit(solution)/shard_map/all_gather | solution.py:171
  703.3 3.1 fusion.41
  707.4 60.2 %all-gather.12.cloned.1.call-done = bf16[2048,768]{1,0:T(8,128)(2,1)} async-done(((bf16[512,768]{1,0:T(8,128)(2,1)}), bf16[2048,768]{1,0:T(8,128)(2,1)}) %all-gather.12.cloned.1.call-update) | async-done | bytes 3145744 | tf_op jit(solution)/shard_map/all_gather | solution.py:170
  767.6 3.2 fusion.40
  772.3 1.4 copy.60
  773.6 2.4 stack.26
  776.1 3.3 fusion.45
  779.4 1.4 copy.68
  780.8 2.1 stack.30
  783.0 3.9 multiply_reduce_fusion.1
  788.8 3.3 multiply_convert_fusion.2
  793.7 1.4 copy.63
  795.1 2.1 stack.28
  797.3 2.6 fusion.49
  801.6 2.3 fusion.46
  803.8 1.4 copy.55
  805.2 2.1 stack.24
  807.4 2.6 fusion.47
  810.0 1.4 copy.57
  811.4 2.3 stack.25
  817.0 2.7 fusion.85
  819.7 4.5 bitcast_add_fusion
  824.3 7.9 fusion.50
  832.2 7.6 fusion.77
  839.9 2.5 fusion.80
  842.7 3.6 fusion.52
  846.4 1.6 fusion.56
  848.0 5.3 fusion.7
  853.4 3.2 fusion.9
  856.7 2.8 add_convert_fusion
  859.5 82.4 %reduce-scatter.14.cloned.1.call-done = f32[512,768]{1,0:T(8,128)} async-done(((f32[2048,768]{1,0:T(8,128)}), f32[512,768]{1,0:T(8,128)}) %reduce-scatter.14.cloned.1.call-update) | async-done | bytes 1572880 | tf_op jit(solution)/shard_map/reduce_scatter | solution.py:197
  941.8 3.9 fusion.37
  945.8 41.2 %all-reduce = (f32[768]{0:T(1024)}, f32[768]{0:T(1024)}, f32[768]{0:T(1024)}) all-reduce(f32[768]{0:T(1024)S(1)} %get-tuple-element.14, f32[768]{0:T(1024)S(1)} %get-tuple-element.27, f32[768]{0:T(1024)S(1)} %get-tuple-element.12), channel_id=1, replica_groups=mesh['dp'=8,'mp'=4] {'dp','mp'}, use_global_device_ids=true, to_apply=%region_20.21 | all-reduce | flops 2304 | bytes 18432 | tf_op jit(solution)/shard_map/psum | solution.py:206
  987.0 2.8 fusion.36
  989.8 93.4 %all-reduce.5.cloned.1.call-done = f32[768,768]{1,0:T(8,128)} async-done(((f32[768,768]{1,0:T(8,128)}), f32[768,768]{1,0:T(8,128)}) %all-reduce.5.cloned.1.call-update) | async-done | bytes 2359312 | tf_op jit(solution)/shard_map/psum | solution.py:206
  1083.2 144.4 %all-reduce.7.cloned.1.call-done = (f32[3,192,768]{2,1,0:T(8,128)}, f32[3,192,768]{2,1,0:T(8,128)}, f32[192,768]{1,0:T(8,128)}, f32[192,768]{1,0:T(8,128)}, f32[768,768]{1,0:T(8,128)}, /*index=5*/f32[768,768]{1,0:T(8,128)}) async-done(((f32[3,192,768]{2,1,0:T(8,128)}, f32[3,192,768]{2,1,0:T(8,128)}, f32[192,768]{1,0:T(8,128)}, f32[192,768]{1,0:T(8,128)}, f32[768,768]{1,0:T(8,128)}, ...) | async-done | bytes 9437200 | tf_op jit(solution)/shard_map/psum | solution.py:203
  1227.6 2.9 copy.158
  1233.4 1.4 copy.162
  1234.9 1.4 copy.163
  1237.4 1.4 copy.164
  (218 shorter events, 35.8 us)
Async XLA Ops:
  7.2 499.0 %copy-start = (bf16[768,768]{1,0:T(8,128)(2,1)S(1)}, bf16[768,768]{1,0:T(8,128)(2,1)}, u32[]{:S(2)}) copy-start(bf16[768,768]{1,0:T(8,128)(2,1)} %param.23) | copy-start | bytes 3538948
  7.2 6.1 copy-start.60
  7.2 72.4 %copy-start.68 = (bf16[3,192,768]{2,1,0:T(8,128)(2,1)S(1)}, bf16[3,192,768]{2,1,0:T(8,128)(2,1)}, u32[]{:S(2)}) copy-start(bf16[3,192,768]{2,1,0:T(8,128)(2,1)} %param.17) | copy-start | bytes 2654212
  7.2 72.4 %all-gather.6.cloned.1.call-start = ((), (), s32[]{:S(2)}) async-start(), calls=%async_computation.5 | async-start | bytes 3932160 | tf_op jit(solution)/shard_map/all_gather | solution.py:120
  13.2 189.9 %reduce-scatter.8.cloned.1.call-start = ((), (), s32[]{:S(2)}) async-start(), calls=%async_computation.7 | async-start | bytes 7864320 | tf_op jit(solution)/shard_map/reduce_scatter | solution.py:127
  13.9 73.5 %copy-start.19 = (pred[16,128,128]{1,2,0:T(8,128)(4,1)}, pred[16,128,128]{1,2,0:T(8,128)(4,1)S(1)}, u32[]{:S(2)}) copy-start(pred[16,128,128]{1,2,0:T(8,128)(4,1)S(1)} %get-tuple-element.39) | copy-start | bytes 786436
  13.9 88.7 %copy-start.17 = (pred[16,128,128]{1,2,0:T(8,128)(4,1)}, pred[16,128,128]{1,2,0:T(8,128)(4,1)S(1)}, u32[]{:S(2)}) copy-start(pred[16,128,128]{1,2,0:T(8,128)(4,1)S(1)} %get-tuple-element.38) | copy-start | bytes 786436
  84.7 2.8 copy-start.36
  86.5 2.0 copy-start.4
  87.5 2.4 copy-start.53
  93.6 223.2 %reduce-scatter.6.cloned.1.call-start = ((), (), s32[]{:S(2)}) async-start(), calls=%async_computation.6 | async-start | bytes 7864320 | tf_op jit(solution)/shard_map/reduce_scatter | solution.py:126
  99.8 2.8 copy-start.37
  101.6 2.0 copy-start.6
  102.6 2.4 copy-start.55
  108.7 208.1 %copy-start.10 = (bf16[512,768]{1,0:T(8,128)(2,1)S(1)}, bf16[512,768]{1,0:T(8,128)(2,1)}, u32[]{:S(2)}) copy-start(bf16[512,768]{1,0:T(8,128)(2,1)} %param.13) | copy-start | bytes 2359300
  108.7 273.6 %all-gather.10.cloned.1.call-start = ((), (), s32[]{:S(2)}) async-start(), calls=%async_computation.10 | async-start | bytes 3932160 | tf_op jit(solution)/shard_map/all_gather | solution.py:147
  109.3 388.4 %all-gather.8.cloned.1.call-start = ((), (), s32[]{:S(2)}) async-start(), calls=%async_computation.8 | async-start | bytes 7864320 | tf_op jit(solution)/shard_map/all_gather | solution.py:134
  109.3 212.9 %copy-start.62 = (bf16[768]{0:T(1024)(128)(2,1)S(1)}, bf16[768]{0:T(1024)(128)(2,1)}, u32[]{:S(2)}) copy-start(bf16[768]{0:T(1024)(128)(2,1)} %param.22) | copy-start | bytes 4612
  109.3 272.9 %copy-start.65 = (bf16[768,768]{1,0:T(8,128)(2,1)S(1)}, bf16[768,768]{1,0:T(8,128)(2,1)}, u32[]{:S(2)}) copy-start(bf16[768,768]{1,0:T(8,128)(2,1)} %param.24) | copy-start | bytes 3538948
  321.9 308.5 %reduce-scatter.12.cloned.1.call-start = ((), (), s32[]{:S(2)}) async-start(), calls=%async_computation.11 | async-start | bytes 7864320 | tf_op jit(solution)/shard_map/reduce_scatter | solution.py:157
  500.8 4.6 copy-start.2
  500.9 5.8 slice-start
  505.4 2.1 slice-start.1
  507.6 7.5 copy-start.3
  521.2 111.6 %copy-start.21 = (bf16[512,768]{1,0:T(8,128)(2,1)S(1)}, bf16[512,768]{1,0:T(8,128)(2,1)}, u32[]{:S(2)}) copy-start(bf16[512,768]{1,0:T(8,128)(2,1)} %param.25) | copy-start | bytes 2359300
  521.2 182.1 %all-gather.14.cloned.1.call-start = ((), (), s32[]{:S(2)}) async-start(), calls=%async_computation.13 | async-start | bytes 3932160 | tf_op jit(solution)/shard_map/all_gather | solution.py:171
  630.4 2.5 copy-start.16
  632.9 4.7 copy-start.15
  639.1 128.5 %all-gather.12.cloned.1.call-start = ((), (), s32[]{:S(2)}) async-start(), calls=%async_computation.12 | async-start | bytes 3932160 | tf_op jit(solution)/shard_map/all_gather | solution.py:170
  639.9 216.8 %reduce-scatter.10.cloned.1.call-start = ((), (), s32[]{:S(2)}) async-start(), calls=%async_computation.9 | async-start | bytes 3932160 | tf_op jit(solution)/shard_map/reduce_scatter | solution.py:143
  649.0 54.3 %copy-start.54 = (bf16[192,768]{1,0:T(8,128)(2,1)S(1)}, bf16[192,768]{1,0:T(8,128)(2,1)}, u32[]{:S(2)}) copy-start(bf16[192,768]{1,0:T(8,128)(2,1)} %param.19) | copy-start | bytes 884740
  649.0 292.8 %reduce-scatter.14.cloned.1.call-start = ((), (), s32[]{:S(2)}) async-start(), calls=%async_computation.14 | async-start | bytes 7864320 | tf_op jit(solution)/shard_map/reduce_scatter | solution.py:197
  707.4 63.6 %copy-start.18 = (pred[16,128,128]{1,2,0:T(8,128)(4,1)S(1)}, pred[16,128,128]{1,2,0:T(8,128)(4,1)}, u32[]{:S(2)}) copy-start(pred[16,128,128]{1,2,0:T(8,128)(4,1)} %copy-done.17) | copy-start | bytes 786436
  707.4 63.6 %copy-start.52 = (f32[16,3,128]{2,1,0:T(4,128)S(1)}, f32[16,3,128]{2,1,0:T(4,128)}, u32[]{:S(2)}) copy-start(f32[16,3,128]{2,1,0:T(4,128)} %copy-done.51) | copy-start | bytes 73732
  767.6 3.4 copy-start.7
  771.0 5.0 copy-start.20
  771.1 5.0 copy-start.50
  783.0 3.9 copy-start.8
  783.0 3.9 copy-start.38
  783.0 3.9 copy-start.40
  788.8 4.4 copy-start.26
  793.2 4.1 copy-start.24
  801.6 5.8 copy-start.28
  810.0 3.7 copy-start.33
  813.8 2.0 copy-start.30
  817.0 2.7 copy-start.56
  817.0 2.7 copy-start.69
  824.3 259.0 %all-reduce.5.cloned.1.call-start = ((), (), s32[]{:S(2)}) async-start(), calls=%async_computation.15 | async-start | bytes 4718592 | tf_op jit(solution)/shard_map/psum | solution.py:206
  824.3 7.9 copy-start.64
  832.2 7.6 copy-start.45
  839.9 2.8 copy-start.12
  842.4 385.2 %all-reduce.7.cloned.1.call-start = ((), (), s32[]{:S(2)}) async-start(), calls=%async_computation.16 | async-start | bytes 18874368 | tf_op jit(solution)/shard_map/psum | solution.py:203
  842.7 3.7 copy-start.14
  842.7 3.7 copy-start.22
  848.0 5.4 copy-start.59
  848.0 5.4 copy-start.63
  856.6 85.2 %copy-start.46 = (bf16[512,768]{1,0:T(8,128)(2,1)S(1)}, bf16[512,768]{1,0:T(8,128)(2,1)}, u32[]{:S(2)}) copy-start(bf16[512,768]{1,0:T(8,128)(2,1)} %get-tuple-element.28) | copy-start | bytes 2359300
  1227.6 3.0 copy-start.44
  1227.6 4.2 copy-start.48
  1230.6 2.0 copy-start.47
  1230.6 2.8 copy-start.41
  1232.6 2.3 copy-start.43
  1234.9 2.5 copy-start.42
  1234.9 3.9 copy-start.1
  (20 other events, 27.7 us)
Sparse Core Ops, SparseCore 0:
  13.4 66.1 all-gather.5
  93.7 109.3 reduce-scatter.7
  205.4 111.2 reduce-scatter.5
  318.2 64.0 all-gather.9
  383.7 113.9 all-gather.7
  521.3 108.9 reduce-scatter.11
  639.2 64.0 all-gather.13
  705.4 62.1 all-gather.11
  769.9 58.8 reduce-scatter.9
  831.0 110.7 reduce-scatter.13
  947.4 135.7 all-reduce.4
  1088.8 138.7 all-reduce.6
where the time goes:
time: 1250 us
  waiting for transfers between devices  986 us (79%)
  matrix products  119 us (10%)
  local copies, waits for them, and re-layouts  49.1 us (4%)
  blocking collectives  41.2 us (3%)
  other arithmetic  33.6 us (3%)
  between operations  15.5 us (1%)
    psum x1, waiting for transfers between devices, body(): lax.psum((grad_self_qkv, grad_cross_qkv, grad_self_out, grad_cross_out, g...  144 us
    reduce_scatter x1, waiting for transfers between devices, body(): lax.psum_scatter(self_part, 'mp', scatter_dimension=0, tiled=True)  114 us
    reduce_scatter x1, waiting for transfers between devices, body(): lax.psum_scatter(grad_normed_two_part, 'mp', scatter_dimension=0, tiled=T...  109 us
    all_gather x1, waiting for transfers between devices, body(): full_mid = lax.all_gather(middle, 'mp', axis=0, tiled=True)  108 us
    reduce_scatter x1, waiting for transfers between devices, body(): lax.psum_scatter(cross_part, 'mp', scatter_dimension=0, tiled=True)  93.8 us
    psum x1, waiting for transfers between devices, body(): lax.psum((grad_gain_one, grad_gate_weight, grad_gate_bias, grad_gain_two)...  93.4 us
    reduce_scatter x1, waiting for transfers between devices, body(): lax.psum_scatter(grad_normed_part, 'mp', scatter_dimension=0, tiled=True)  82.4 us
    all_gather x1, waiting for transfers between devices, body(): normed = lax.all_gather(normed_own, 'mp', axis=0, tiled=True)  65.7 us
  transfers between devices with their start and end apart: 12, of which 11 were waited for; matrix products, arithmetic and copies ran while one was open for 11% of the time, Pallas kernels for 0%

commit v1 on v0

v1 whole, which is shorter than its diff:
```python
import functools

import jax
import jax.numpy as jnp
from jax import lax
from jax.experimental import pallas as pl
from jax.experimental.pallas import tpu as pltpu
from jax.sharding import PartitionSpec as P

HEAD = 64
LANG = 96
SLOTS = 128
EPS = 1e-5
NEG = -1e30
GC = 0.7978845608028654
GK = 0.044715
f32 = jnp.float32
bf16 = jnp.bfloat16
MESH = pl.DeviceIdType.MESH


def mm(lhs, rhs, form):
    dims = {"nn": ((1,), (0,)), "nt": ((1,), (1,)), "tn": ((0,), (0,))}[form]
    return lax.dot_general(lhs, rhs, (dims, ((), ())), preferred_element_type=f32)


def blk(start, size, align):
    return pl.ds(pl.multiple_of(start, align), size)


def standardize(rows):
    centre = jnp.mean(rows, axis=1, keepdims=True)
    offset = rows - centre
    spread = jnp.mean(offset * offset, axis=1, keepdims=True)
    inv = lax.rsqrt(spread + EPS)
    return offset * inv, inv


def layer_kernel(
    x_ref, og_ref, bias_ref, again_ref, fgain_ref, gate_ref, gbias_ref,
    sq_ref, cq_ref, so_ref, co_ref, up_ref, dn_ref,
    out_ref, tg_ref, fin, gout, vec_ref,
    buf, crecv, p1a, p1b, p2a, p2b, zrv, gg, gcr, gxr, gyr, gzr, vs, vr, vz,
    h, qkv, o, lse, sc, aa, mid, h2, acc, gh, eb, wb, gz,
    loc, az_s, az_r, a1_s, a1_r, a2_s, a2_r, ac_s, ac_r,
    rc_s, rc_r, r1_s, r1_r, r2_s, r2_r, rz_s, rz_r,
    f1_s, f1_r, f2_s, f2_r, fc_s, fc_r, fl,
    g_s, g_r, gz_s, gz_r, ga_s, ga_r, gl, v_s, v_r, vz_s, vz_r,
):
    R, D = x_ref.shape
    CH = buf.shape[3]
    XH, YH = CH // 2, D // 2
    AR = XH // 2
    QR = sq_ref.shape[0]
    F = QR // 3
    heads = F // HEAD
    pages = R // SLOTS
    GX = gg.shape[2] // 2

    dp = lax.axis_index("dp")
    z = lax.axis_index("mp")
    c = dp % 2
    x = (dp // 2) % 2
    y = (dp // 4) % 2
    s = z // 2
    ismid = (z + s) % 2
    dev_c = (dp + 1 - 2 * c, z)
    dev_x = (dp + 2 - 4 * x, z)
    dev_y = (dp + 4 - 8 * y, z)

    def zof(slot):
        b0, b1 = slot % 2, slot // 2
        near = (1 - b0) * z + b0 * (4 * s + 1 - z)
        far = (1 - b0) * (2 - s) + b0 * (3 - 3 * s)
        return (1 - b1) * near + b1 * far

    def seen_as(slot):
        is1 = 1 - slot // 2
        return is1 + (1 - is1) * (3 - ismid)

    def remote(src, dst, ss, rs, dev):
        return pltpu.make_async_remote_copy(
            src_ref=src, dst_ref=dst, send_sem=ss, recv_sem=rs, device_id=dev, device_id_type=MESH
        )

    bar = pltpu.get_barrier_semaphore()
    partners = (dev_c, dev_x, dev_y, (dp, zof(1)), (dp, zof(2)), (dp, zof(3)))
    for dev in partners:
        pl.semaphore_signal(bar, inc=1, device_id=dev, device_id_type=MESH)

    local = []
    for i, (src, g, cc, r0) in enumerate(
        (
            (sq_ref, 0, 0, 0), (so_ref, 0, 0, QR), (cq_ref, 0, 1, 0), (co_ref, 0, 1, QR),
            (up_ref, 1, 0, 0), (dn_ref, 1, 1, 0),
        )
    ):
        cp = pltpu.make_async_copy(src, buf.at[g, cc, z, pl.ds(r0, src.shape[0]), :], loc.at[i])
        cp.start()
        local.append(cp)

    def wpart(g, cc, zz, r0, nr, c0, nc):
        return buf.at[g, cc, zz, blk(r0, nr, 16), blk(c0, nc, 128)]

    def wquarter(g, zz):
        return wpart(g, c, zz, XH * x, XH, YH * y, YH)

    def z_copy(g, zz, slot_to, sidx, rslot):
        ref = wquarter(g, zz)
        return remote(ref, ref, az_s.at[g, sidx], az_r.at[g, rslot], (dp, zof(slot_to)))

    def ag_zsend(g):
        z_copy(g, z, 1, 0, 1).start()

        @pl.when(ismid == 1)
        def _():
            z_copy(g, z, 2, 1, 2).start()

    def ag_zsend_wait(g):
        z_copy(g, z, 1, 0, 1).wait_send()

        @pl.when(ismid == 1)
        def _():
            for i in range(1, 5):
                z_copy(g, z, 1, i, 1).wait_send()

    def ag_p1(g, j):
        zz = zof(j)
        ra = wpart(g, c, zz, XH * x, AR, YH * y, YH)
        rb = wpart(g, c, zz, XH * x + AR, AR, YH * y, YH)
        ia = wpart(g, c, zz, XH * (1 - x), AR, YH * y, YH)
        ib = wpart(g, c, zz, XH * x + AR, AR, YH * (1 - y), YH)
        return (
            (remote(ra, ra, a1_s.at[g, j, 0], a1_r.at[g, j, 0], dev_x),
             remote(rb, rb, a1_s.at[g, j, 1], a1_r.at[g, j, 1], dev_y)),
            (remote(ia, ia, a1_s.at[g, j, 0], a1_r.at[g, j, 0], dev_x),
             remote(ib, ib, a1_s.at[g, j, 1], a1_r.at[g, j, 1], dev_y)),
        )

    def ag_p2(g, j):
        zz = zof(j)
        outs, ins = [], []
        for xx in range(2):
            ra = wpart(g, c, zz, XH * xx, AR, YH * y, YH)
            ia = wpart(g, c, zz, XH * xx, AR, YH * (1 - y), YH)
            outs.append(remote(ra, ra, a2_s.at[g, j, xx], a2_r.at[g, j, xx], dev_y))
            ins.append(remote(ia, ia, a2_s.at[g, j, xx], a2_r.at[g, j, xx], dev_y))
        rb = wpart(g, c, zz, XH * x + AR, AR, 0, D)
        ib = wpart(g, c, zz, XH * (1 - x) + AR, AR, 0, D)
        outs.append(remote(rb, rb, a2_s.at[g, j, 2], a2_r.at[g, j, 2], dev_x))
        ins.append(remote(ib, ib, a2_s.at[g, j, 2], a2_r.at[g, j, 2], dev_x))
        return outs, ins

    def ag_c(g, j):
        zz = zof(j)
        mine, theirs = buf.at[g, c, zz], buf.at[g, 1 - c, zz]
        return (
            remote(mine, mine, ac_s.at[g, j], ac_r.at[g, j], dev_c),
            remote(theirs, theirs, ac_s.at[g, j], ac_r.at[g, j], dev_c),
        )

    def pump_ag(t):
        @pl.when(t < 6)
        def _():
            g, j = t // 3, t % 3 + 1
            z_copy(g, zof(j), 1, 0, j).wait_recv()

            @pl.when(ismid == 1)
            def _():
                is1 = 1 - j // 2
                z_copy(g, zof(j), 2 * is1 + 1 - is1, j + 1, 3 * is1 + j * (1 - is1)).start()

            for cp in ag_p1(g, j)[0]:
                cp.start()

        @pl.when((t >= 1) & (t < 7))
        def _():
            g, j = (t - 1) // 3, (t - 1) % 3 + 1
            outs, ins = ag_p1(g, j)
            for cp in ins:
                cp.wait_recv()
            for cp in ag_p2(g, j)[0]:
                cp.start()
            for cp in outs:
                cp.wait_send()

        @pl.when((t >= 2) & (t < 8))
        def _():
            g, j = (t - 2) // 3, (t - 2) % 3 + 1
            outs, ins = ag_p2(g, j)
            for cp in ins:
                cp.wait_recv()
            ag_c(g, j)[0].start()
            for cp in outs:
                cp.wait_send()

    def ag_done(g, j):
        mine, theirs = ag_c(g, j)
        theirs.wait_recv()
        mine.wait_send()

    def add_rows(dst, dst_idx, r0, nr, c0, nc, src, src_idx):
        step = 64 if nr % 64 == 0 else 48

        @pl.loop(0, nr // step)
        def _(i):
            rows = blk(r0 + i * step, step, 16)
            cols = blk(c0, nc, 128)
            d = dst[(*dst_idx, rows, cols)].astype(f32)
            t = src[(*src_idx, blk(i * step, step, 16), slice(None))].astype(f32)
            dst[(*dst_idx, rows, cols)] = (d + t).astype(bf16)

    def rs_c(n):
        return remote(buf.at[2 - n // 4, 1 - c, n % 4], crecv.at[n % 4], rc_s.at[n], rc_r.at[n], dev_c)

    def rs_p1(n):
        b, k = 2 - n // 4, n % 4
        cps = [remote(buf.at[b, c, k, blk(XH * (1 - x), AR, 16), :], p1a.at[k], r1_s.at[n, 0], r1_r.at[n, 0], dev_x)]
        for xx in range(2):
            cps.append(
                remote(
                    buf.at[b, c, k, pl.ds(XH * xx + AR, AR), blk(YH * (1 - y), YH, 128)],
                    p1b.at[k, xx], r1_s.at[n, 1 + xx], r1_r.at[n, 1 + xx], dev_y,
                )
            )
        return cps

    def rs_p2(n):
        b, k = 2 - n // 4, n % 4
        return [
            remote(
                buf.at[b, c, k, blk(XH * x, AR, 16), blk(YH * (1 - y), YH, 128)],
                p2a.at[k], r2_s.at[n, 0], r2_r.at[n, 0], dev_y,
            ),
            remote(
                buf.at[b, c, k, blk(XH * (1 - x) + AR, AR, 16), blk(YH * y, YH, 128)],
                p2b.at[k], r2_s.at[n, 1], r2_r.at[n, 1], dev_x,
            ),
        ]

    def rs_z(n, rslot):
        b, k, g = 2 - n // 4, n % 4, n // 4
        return remote(
            buf.at[b, c, k, blk(XH * x, XH, 16), blk(YH * y, YH, 128)],
            zrv.at[g, rslot - 1], rz_s.at[n], rz_r.at[g, rslot], (dp, zof(k)),
        )

    def pump_rs(t):
        def chunk(v):
            return v - v // 5

        def has(v):
            return (v >= 0) & (v < 9) & (v != 4)

        @pl.when(has(t))
        def _():
            rs_c(chunk(t)).start()

        @pl.when(has(t - 1))
        def _():
            n = chunk(t - 1)
            cp = rs_c(n)
            cp.wait_recv()
            add_rows(buf, (2 - n // 4, c, n % 4), 0, CH, 0, D, crecv, (n % 4,))
            for q in rs_p1(n):
                q.start()
            cp.wait_send()

        @pl.when(has(t - 2))
        def _():
            n = chunk(t - 2)
            idx = (2 - n // 4, c, n % 4)
            cps = rs_p1(n)
            for q in cps:
                q.wait_recv()
            add_rows(buf, idx, XH * x, AR, 0, D, p1a, (n % 4,))
            for xx in range(2):
                add_rows(buf, idx, XH * xx + AR, AR, YH * y, YH, p1b, (n % 4, xx))
            for q in rs_p2(n):
                q.start()
            for q in cps:
                q.wait_send()

        @pl.when(has(t - 3))
        def _():
            n = chunk(t - 3)
            idx = (2 - n // 4, c, n % 4)
            cps = rs_p2(n)
            for q in cps:
                q.wait_recv()
            add_rows(buf, idx, XH * x, AR, YH * y, YH, p2a, (n % 4,))
            add_rows(buf, idx, XH * x + AR, AR, YH * y, YH, p2b, (n % 4,))

            @pl.when(n % 4 != 0)
            def _():
                rs_z(n, seen_as(n % 4)).start()

            for q in cps:
                q.wait_send()

    def fin_part(g, r0, nr, c0, nc):
        return fin.at[g, c, blk(r0, nr, 16), blk(c0, nc, 128)]

    def fin_p1(g):
        b = 2 - g
        return [
            remote(
                buf.at[b, c, 0, blk(XH * x, AR, 16), blk(YH * y, YH, 128)],
                fin_part(g, XH * x, AR, YH * y, YH), f1_s.at[g, 0], f1_r.at[g, 0], dev_x,
            ),
            remote(
                buf.at[b, c, 0, blk(XH * x + AR, AR, 16), blk(YH * y, YH, 128)],
                fin_part(g, XH * x + AR, AR, YH * y, YH), f1_s.at[g, 1], f1_r.at[g, 1], dev_y,
            ),
        ]

    def fin_local(g):
        return pltpu.make_async_copy(
            buf.at[2 - g, c, 0, blk(XH * x, XH, 16), blk(YH * y, YH, 128)],
            fin_part(g, XH * x, XH, YH * y, YH), fl.at[g],
        )

    def fin_p2(g):
        cps = []
        for xx in range(2):
            ref = fin_part(g, XH * xx, AR, YH * y, YH)
            cps.append(remote(ref, ref, f2_s.at[g, xx], f2_r.at[g, xx], dev_y))
        ref = fin_part(g, XH * x + AR, AR, 0, D)
        cps.append(remote(ref, ref, f2_s.at[g, 2], f2_r.at[g, 2], dev_x))
        return cps

    def fin_c(g):
        return remote(fin.at[g, c], fin.at[g, c], fc_s.at[g], fc_r.at[g], dev_c)

    def fin_step0(g):
        b = 2 - g
        for slot in range(1, 4):
            rs_z(4 * g + slot, slot).wait_recv()
        for i in range(XH // 64):
            rows = blk(XH * x + 64 * i, 64, 16)
            cols = blk(YH * y, YH, 128)
            t = buf[b, c, 0, rows, cols].astype(f32)
            for slot in range(3):
                t = t + zrv[g, slot, pl.ds(64 * i, 64), :].astype(f32)
            buf[b, c, 0, rows, cols] = t.astype(bf16)
        fin_local(g).start()
        for q in fin_p1(g):
            q.start()
        for slot in range(1, 4):
            rs_z(4 * g + slot, slot).wait_send()

    def fin_step1(g):
        for q in fin_p1(g):
            q.wait_recv()
        fin_local(g).wait()
        for q in fin_p2(g):
            q.start()
        for q in fin_p1(g):
            q.wait_send()

    def fin_step2(g):
        for q in fin_p2(g):
            q.wait_recv()
        fin_c(g).start()
        for q in fin_p2(g):
            q.wait_send()

    def fin_step3(g):
        fin_c(g).wait_recv()
        fin_c(g).wait_send()

    def g_copy(i):
        xs, xo = blk(GX * x, GX, 16), blk(GX * (1 - x), GX, 16)
        ys, yo = blk(YH * y, YH, 128), blk(YH * (1 - y), YH, 128)
        src, dst, dev = {
            0: lambda: (gg.at[:, 1 - c], gcr, dev_c),
            1: lambda: (gg.at[:, c, xo, :], gxr, dev_x),
            2: lambda: (gg.at[:, c, xs, yo], gyr, dev_y),
            3: lambda: (gout.at[:, c, xs, ys], gout.at[:, c, xs, ys], dev_y),
            4: lambda: (gout.at[:, c, xs, :], gout.at[:, c, xs, :], dev_x),
            5: lambda: (gout.at[:, c], gout.at[:, c], dev_c),
        }[i]()
        return remote(src, dst, g_s.at[i], g_r.at[i], dev)

    def g_z(slot, rslot):
        src = gg.at[zof(slot), c, blk(GX * x, GX, 16), blk(YH * y, YH, 128)]
        return remote(src, gzr.at[rslot - 1], gz_s.at[slot], gz_r.at[rslot], (dp, zof(slot)))

    def g_za(slot, rslot):
        src = gg.at[z, c, blk(GX * x, GX, 16), blk(YH * y, YH, 128)]
        dst = gout.at[z, c, blk(GX * x, GX, 16), blk(YH * y, YH, 128)]
        return remote(src, dst, ga_s.at[slot], ga_r.at[rslot], (dp, zof(slot)))

    def g_local():
        src = gg.at[z, c, blk(GX * x, GX, 16), blk(YH * y, YH, 128)]
        dst = gout.at[z, c, blk(GX * x, GX, 16), blk(YH * y, YH, 128)]
        return pltpu.make_async_copy(src, dst, gl.at[0])

    def g_step(i):
        xs, ys = blk(GX * x, GX, 16), blk(YH * y, YH, 128)
        if i == 0:
            g_copy(0).start()
        if i == 1:
            g_copy(0).wait_recv()
            for q in range(4):
                add_rows(gg, (q, c), 0, 2 * GX, 0, D, gcr, (q,))
            g_copy(1).start()
            g_copy(0).wait_send()
        if i == 2:
            g_copy(1).wait_recv()
            for q in range(4):
                add_rows(gg, (q, c), GX * x, GX, 0, D, gxr, (q,))
            g_copy(2).start()
            g_copy(1).wait_send()
        if i == 3:
            g_copy(2).wait_recv()
            for q in range(4):
                add_rows(gg, (q, c), GX * x, GX, YH * y, YH, gyr, (q,))
            for slot in range(1, 4):
                g_z(slot, seen_as(slot)).start()
            g_copy(2).wait_send()
        if i == 4:
            for slot in range(1, 4):
                g_z(slot, slot).wait_recv()
            t = gg[z, c, xs, ys].astype(f32)
            for slot in range(3):
                t = t + gzr[slot].astype(f32)
            gg[z, c, xs, ys] = t.astype(bf16)
            g_local().start()
            for slot in range(1, 4):
                g_za(slot, seen_as(slot)).start()
            for slot in range(1, 4):
                g_z(slot, slot).wait_send()
        if i == 5:
            for slot in range(1, 4):
                g_za(slot, slot).wait_recv()
            g_local().wait()
            g_copy(3).start()
            for slot in range(1, 4):
                g_za(slot, slot).wait_send()
        if i == 6:
            g_copy(3).wait_recv()
            g_copy(4).start()
            g_copy(3).wait_send()
        if i == 7:
            g_copy(4).wait_recv()
            g_copy(5).start()
            g_copy(4).wait_send()
        if i == 8:
            g_copy(5).wait_recv()
            g_copy(5).wait_send()

    def v_copy(i):
        return remote(vs.at[i], vr.at[i], v_s.at[i], v_r.at[i], (dev_c, dev_x, dev_y)[i])

    def v_z(slot, zz_dst, rslot):
        return remote(vz.at[z], vz.at[zz_dst], vz_s.at[slot], vz_r.at[rslot], (dp, zof(slot)))

    def v_step(i):
        if i == 0:
            v_copy(0).start()
        if i in (1, 2):
            v_copy(i - 1).wait_recv()
            vs[i] = vs[i - 1] + vr[i - 1]
            v_copy(i).start()
            v_copy(i - 1).wait_send()
        if i == 3:
            v_copy(2).wait_recv()
            vz[z] = vs[2] + vr[2]
            for slot in range(1, 4):
                v_z(slot, z, seen_as(slot)).start()
            v_copy(2).wait_send()
        if i == 4:
            for slot in range(1, 4):
                v_z(slot, z, slot).wait_recv()
            vec_ref[...] = (vz[0] + vz[1]) + (vz[2] + vz[3])
            for slot in range(1, 4):
                v_z(slot, z, slot).wait_send()

    pl.semaphore_wait(bar, 6)
    for cp in local[:4]:
        cp.wait()
    ag_zsend(0)

    TR = 64
    again = again_ref[...].astype(f32)
    fgain = fgain_ref[...].astype(f32)
    gbias = gbias_ref[...].astype(f32)

    @pl.loop(0, R // TR)
    def _(i):
        rows = blk(i * TR, TR, 16)
        u, _inv = standardize(x_ref[rows, :].astype(f32))
        h[rows, :] = (u * again).astype(bf16)
        sc[rows, :] = jnp.zeros((TR, D), f32)
        mid[rows, :] = jnp.zeros((TR, D), f32)
        gh[rows, :] = jnp.zeros((TR, D), f32)

    vs[...] = jnp.zeros_like(vs)
    for cp in local[4:]:
        cp.wait()
    ag_zsend(1)
    pump_ag(0)

    @pl.loop(0, R // 128)
    def _(i):
        rows = blk(i * 128, 128, 16)
        aa[rows, :] = jax.nn.sigmoid(mm(h[rows, :], gate_ref[...], "nn") + gbias)

    pump_ag(1)

    @pl.loop(0, 4)
    def _(k):
        zz = zof(k)

        @pl.when(k > 0)
        def _():
            ag_done(0, k)

        for at in range(2):
            qkv[at, k] = mm(buf[0, at, zz, 0:QR, :], h[...], "nt").astype(bf16)

        @pl.loop(0, pages)
        def _(p):
            cols = blk(p * SLOTS, SLOTS, 128)
            for at in range(2):
                for hh in range(heads):
                    qt = qkv[at, k, HEAD * hh : HEAD * (hh + 1), cols]
                    kt = qkv[at, k, F + HEAD * hh : F + HEAD * (hh + 1), cols]
                    vt = qkv[at, k, 2 * F + HEAD * hh : 2 * F + HEAD * (hh + 1), cols]
                    st = mm(kt, qt, "tn") * HEAD ** (-0.5) + bias_ref[at, p]
                    top = jnp.max(st, axis=0, keepdims=True)
                    ex = jnp.exp(st - top)
                    tot = jnp.sum(ex, axis=0, keepdims=True)
                    pt = (ex * (1.0 / tot)).astype(bf16)
                    lse[at, k, hh : hh + 1, cols] = top + jnp.log(tot)
                    o[at, k, HEAD * hh : HEAD * (hh + 1), cols] = mm(vt, pt, "nn").astype(bf16)

        for at, dst in ((0, sc), (1, mid)):
            dst[...] += mm(o[at, k], buf[0, at, zz, QR:CH, :], "tn")
        pump_ag(k + 2)

    ag_zsend_wait(0)

    @pl.loop(0, R // TR)
    def _(i):
        rows = blk(i * TR, TR, 16)
        a = aa[rows, :]
        sv, cv = sc[rows, :], mid[rows, :]
        mv = x_ref[rows, :].astype(f32) + a * sv + (1.0 - a) * cv
        sc[rows, :] = sv - cv
        mid[rows, :] = mv
        acc[rows, :] = mv
        u, _inv = standardize(mv)
        h2[rows, :] = (u * fgain).astype(bf16)

    @pl.loop(0, 4)
    def _(k):
        zz = zof(k)

        @pl.when(k > 0)
        def _():
            ag_done(1, k)

        MT = 256

        @pl.loop(0, R // MT)
        def _(i):
            rows = blk(i * MT, MT, 16)
            w = mm(h2[rows, :], buf[1, 0, zz], "nn")
            ge = mm(og_ref[rows, :], buf[1, 1, zz], "nt")
            w2 = w * w
            th = jnp.tanh(GC * w * (1.0 + GK * w2))
            half = 0.5 * (1.0 + th)
            eb[rows, :] = (w * half).astype(bf16)
            dg = half + 0.5 * w * (1.0 - th * th) * (GC * (1.0 + 3.0 * GK * w2))
            wb[rows, :] = (dg * ge).astype(bf16)

        @pl.loop(0, R // MT)
        def _(i):
            rows = blk(i * MT, MT, 16)
            acc[rows, :] += mm(eb[rows, :], buf[1, 1, zz], "nn")
            gh[rows, :] += mm(wb[rows, :], buf[1, 0, zz], "nt")

        @pl.loop(0, CH // 256)
        def _(i):
            cols = blk(i * 256, 256, 128)
            buf[2, 1, k, blk(i * 256, 256, 16), :] = mm(eb[:, cols], og_ref[...], "tn").astype(bf16)
            buf[2, 0, k, blk(i * 256, 256, 16), :] = mm(h2[:, cols], wb[...], "tn").astype(bf16)

        pump_rs(k)

        @pl.when(k < 2)
        def _():
            pump_ag(k + 6)

    ag_zsend_wait(1)

    TS = 32
    zero_row = jnp.zeros((1, D), f32)

    def mid_back(i, sums):
        gain_sum, bias_sum = sums
        rows = blk(i * TS, TS, 16)
        ov = acc[rows, :]
        out_ref[rows, :] = ov.astype(bf16)
        u, inv = standardize(mid[rows, :])
        gy = gh[rows, :]
        gain_sum = gain_sum + jnp.sum(gy * u, axis=0, keepdims=True)
        sy = gy * fgain
        m1 = jnp.mean(sy, axis=1, keepdims=True)
        m2 = jnp.mean(sy * u, axis=1, keepdims=True)
        gm = og_ref[rows, :].astype(f32) + inv * (sy - m1 - u * m2)
        acc[rows, :] = gm
        gh[rows, :] = jnp.zeros((TS, D), f32)
        a = aa[rows, :]
        eb[rows, :] = (a * gm).astype(bf16)
        wb[rows, :] = ((1.0 - a) * gm).astype(bf16)
        gzv = (gm * sc[rows, :] * a * (1.0 - a)).astype(bf16)
        gz[rows, :] = gzv
        bias_sum = bias_sum + jnp.sum(gzv.astype(f32), axis=0, keepdims=True)
        return gain_sum, bias_sum

    gain_sum, bias_sum = lax.fori_loop(0, R // TS, mid_back, (zero_row, zero_row))
    vs[0, 1:2, :] = bias_sum
    vs[0, 2:3, :] = gain_sum
    pump_rs(4)

    for i in range(4):
        t = mm(h[:, F * i : F * (i + 1)], gz[...], "tn").astype(bf16)
        gg[i, 0] = t[: F // 2]
        gg[i, 1] = t[F // 2 :]
    g_step(0)

    @pl.loop(0, 4)
    def _(k):
        zz = zof(k)
        for at, gref in ((0, eb), (1, wb)):
            buf[1, at, k, QR:CH, :] = mm(o[at, k], gref[...], "nn").astype(bf16)
            o[at, k] = mm(buf[0, at, zz, QR:CH, :], gref[...], "nt").astype(bf16)

        @pl.loop(0, pages)
        def _(p):
            cols = blk(p * SLOTS, SLOTS, 128)
            for at in range(2):
                for hh in range(heads):
                    qs = slice(HEAD * hh, HEAD * (hh + 1))
                    ks = slice(F + HEAD * hh, F + HEAD * (hh + 1))
                    vsl = slice(2 * F + HEAD * hh, 2 * F + HEAD * (hh + 1))
                    qt = qkv[at, k, qs, cols]
                    kt = qkv[at, k, ks, cols]
                    vt = qkv[at, k, vsl, cols]
                    go = o[at, k, qs, cols]
                    st = mm(kt, qt, "tn") * HEAD ** (-0.5) + bias_ref[at, p]
                    pt = jnp.exp(st - lse[at, k, hh : hh + 1, cols])
                    gvt = mm(go, pt.astype(bf16), "nt")
                    gpt = mm(vt, go, "tn")
                    pg = pt * gpt
                    gst = (pg - pt * jnp.sum(pg, axis=0, keepdims=True)).astype(bf16)
                    gqt = mm(kt, gst, "nn") * HEAD ** (-0.5)
                    gkt = mm(qt, gst, "nt") * HEAD ** (-0.5)
                    qkv[at, k, qs, cols] = gqt.astype(bf16)
                    qkv[at, k, ks, cols] = gkt.astype(bf16)
                    qkv[at, k, vsl, cols] = gvt.astype(bf16)

        for at in range(2):
            buf[1, at, k, 0:QR, :] = mm(qkv[at, k], h[...], "nn").astype(bf16)
        pump_rs(5 + k)
        for i in range(4):

            @pl.when(k == i)
            def _():
                g_step(i + 1)

        for at in range(2):
            gh[...] += mm(qkv[at, k], buf[0, at, zz, 0:QR, :], "tn")

    @pl.loop(0, R // 128)
    def _(i):
        rows = blk(i * 128, 128, 16)
        gh[rows, :] += mm(gz[rows, :], gate_ref[...], "nt")

    def first_back(i, gain_sum):
        rows = blk(i * TS, TS, 16)
        u, inv = standardize(x_ref[rows, :].astype(f32))
        gy = gh[rows, :]
        gain_sum = gain_sum + jnp.sum(gy * u, axis=0, keepdims=True)
        sy = gy * again
        m1 = jnp.mean(sy, axis=1, keepdims=True)
        m2 = jnp.mean(sy * u, axis=1, keepdims=True)
        tg_ref[rows, :] = (acc[rows, :] + inv * (sy - m1 - u * m2)).astype(bf16)
        return gain_sum

    vs[0, 0:1, :] = lax.fori_loop(0, R // TS, first_back, zero_row)
    v_step(0)
    pump_rs(9)
    g_step(5)
    fin_step0(0)
    v_step(1)
    pump_rs(10)
    g_step(6)
    fin_step1(0)
    v_step(2)
    pump_rs(11)
    g_step(7)
    fin_step2(0)
    v_step(3)
    fin_step0(1)
    g_step(8)
    fin_step3(0)
    v_step(4)
    fin_step1(1)
    fin_step2(1)
    fin_step3(1)


def body(
    tokens, region_mask, attn_gain, self_qkv, cross_qkv, self_out, cross_out, gate_weight, gate_bias,
    ffn_gain, up_weight, down_weight, out_grad, *, outer,
):
    R, D = tokens.shape
    F = self_out.shape[0]
    QR = 3 * F
    CH = QR + F
    pages = R // SLOTS
    marks = lax.dynamic_slice_in_dim(region_mask, lax.axis_index("mp") * pages, pages, 0)
    lang = jnp.arange(SLOTS) < LANG
    same = lang[:, None] == lang[None, :]
    real = (marks > 0)[:, :, None]
    bias = jnp.stack([jnp.where(same[None] & real, 0.0, NEG), jnp.where(~same[None] & real, 0.0, NEG)]).astype(f32)

    vm = pl.BlockSpec(memory_space=pltpu.VMEM)
    hb = pl.BlockSpec(memory_space=pl.ANY)
    dma = pltpu.SemaphoreType.DMA
    XH, YH, AR, GX = CH // 2, D // 2, CH // 4, D // 16
    scratch = [
        pltpu.VMEM((3, 2, 4, CH, D), bf16),
        pltpu.VMEM((4, CH, D), bf16),
        pltpu.VMEM((4, AR, D), bf16),
        pltpu.VMEM((4, 2, AR, YH), bf16),
        pltpu.VMEM((4, AR, YH), bf16),
        pltpu.VMEM((4, AR, YH), bf16),
        pltpu.VMEM((2, 3, XH, YH), bf16),
        pltpu.VMEM((4, 2, 2 * GX, D), bf16),
        pltpu.VMEM((4, 2 * GX, D), bf16),
        pltpu.VMEM((4, GX, D), bf16),
        pltpu.VMEM((4, GX, YH), bf16),
        pltpu.VMEM((3, GX, YH), bf16),
        pltpu.VMEM((3, 8, D), f32),
        pltpu.VMEM((3, 8, D), f32),
        pltpu.VMEM((4, 8, D), f32),
        pltpu.VMEM((R, D), bf16),
        pltpu.VMEM((2, 4, QR, R), bf16),
        pltpu.VMEM((2, 4, F, R), bf16),
        pltpu.VMEM((2, 4, 8, R), f32),
        pltpu.VMEM((R, D), f32),
        pltpu.VMEM((R, D), f32),
        pltpu.VMEM((R, D), f32),
        pltpu.VMEM((R, D), bf16),
        pltpu.VMEM((R, D), f32),
        pltpu.VMEM((R, D), f32),
        pltpu.VMEM((R, D), bf16),
        pltpu.VMEM((R, D), bf16),
        pltpu.VMEM((R, D), bf16),
        dma((6,)), dma((2, 5)), dma((2, 4)), dma((2, 4, 2)), dma((2, 4, 2)), dma((2, 4, 3)), dma((2, 4, 3)),
        dma((2, 4)), dma((2, 4)),
        dma((8,)), dma((8,)), dma((8, 3)), dma((8, 3)), dma((8, 2)), dma((8, 2)), dma((8,)), dma((2, 4)),
        dma((2, 2)), dma((2, 2)), dma((2, 3)), dma((2, 3)), dma((2,)), dma((2,)), dma((2,)),
        dma((6,)), dma((6,)), dma((4,)), dma((4,)), dma((4,)), dma((4,)), dma((1,)),
        dma((3,)), dma((3,)), dma((4,)), dma((4,)),
    ]
    out, tg, fin, gout, vec = pl.pallas_call(
        layer_kernel,
        out_shape=(
            jax.ShapeDtypeStruct((R, D), bf16),
            jax.ShapeDtypeStruct((R, D), bf16),
            jax.ShapeDtypeStruct((2, 2, CH, D), bf16),
            jax.ShapeDtypeStruct((4, 2, 2 * GX, D), bf16),
            jax.ShapeDtypeStruct((8, D), f32),
        ),
        in_specs=[vm] * 7 + [hb] * 6,
        out_specs=(vm, vm, hb, hb, vm),
        scratch_shapes=scratch,
        compiler_params=pltpu.CompilerParams(
            collective_id=1, has_side_effects=True, vmem_limit_bytes=64 * 2**20 - 2**17
        ),
    )(
        tokens, out_grad, bias, attn_gain.reshape(1, D), ffn_gain.reshape(1, D), gate_weight, gate_bias.reshape(1, D),
        self_qkv.reshape(QR, D), cross_qkv.reshape(QR, D), self_out, cross_out, up_weight, down_weight,
    )
    grads = (
        vec[0], fin[1, 0, :QR].reshape(3, F, D), fin[1, 1, :QR].reshape(3, F, D), fin[1, 0, QR:], fin[1, 1, QR:],
        gout.reshape(D, D), vec[1], vec[2], fin[0, 0], fin[0, 1],
    )
    grads = tuple(g.astype(f32) for g in grads)
    if outer > 1:
        first = (lax.axis_index("dp") % 8 == 0).astype(f32)
        grads = lax.psum(tuple(g * first for g in grads), "dp")
    return (out, tg) + tuple(grads)


def solution(mesh):
    rows = P(("dp", "mp"), None)
    weights = (P(), P(None, "mp", None), P(None, "mp", None), P("mp", None), P("mp", None), P(), P(), P(), P(None, "mp"), P("mp", None))
    return jax.shard_map(
        functools.partial(body, outer=mesh.shape["dp"] // 8),
        mesh=mesh,
        in_specs=(rows, P("dp", None)) + weights + (rows,),
        out_specs=(rows, rows) + weights,
        check_vma=False,
    )
```

time: 1250 us -> 231 us (0.18)
  waiting for transfers between devices: 986 us -> 0 us
  Pallas kernels: 0 us -> 210 us
  matrix products: 119 us -> 0 us
  blocking collectives: 41.2 us -> 0 us
  local copies, waits for them, and re-layouts: 49.1 us -> 8.59 us
  other arithmetic: 33.6 us -> 10.9 us
  between operations: 15.5 us -> 0.69 us
    reduce_scatter x5 -> x0, waiting for transfers between devices: 399 us -> none  [the longest x1 114 us: body(): lax.psum_scatter(self_part, 'mp', scatter_dimension=0, tiled=True)]
    all_gather x5 -> x0, waiting for transfers between devices: 348 us -> none  [the longest x1 108 us: body(): full_mid = lax.all_gather(middle, 'mp', axis=0, tiled=True)]
    psum x2 -> x0, waiting for transfers between devices: 238 us -> none  [the longest x1 144 us: body(): lax.psum((grad_self_qkv, grad_cross_qkv, grad_self_out, grad_cross_out, g...]
    pallas_call x0 -> x1, Pallas kernels: none -> 210 us  [body(): pl.pallas_call(layer_kernel, out_shape=(jax.ShapeDtypeStruct((R, D), bf16...]
    dot_general x33 -> x0, matrix products: 119 us -> none  [the longest x1 8.59 us: body(): ffn_part = jnp.dot(hidden, down_weight, preferred_element_type=jnp.float32)]
    psum x1 -> x0, blocking collectives: 41.2 us -> none  [body(): lax.psum((grad_gain_one, grad_gate_weight, grad_gate_bias, grad_gain_two)...]
    unnamed x159 -> x10, local copies, waits for them, and re-layouts: 27.1 us -> 1.77 us
    reduce_sum x8 -> x0, other arithmetic: 18.8 us -> none  [the longest x2 5.22 us: standardize(): spread = jnp.mean(offset * offset, axis=1, keepdims=True)]
  transfers between devices with their start and end apart: 12 -> 0, of which waited for: 11 -> 0; matrix products, arithmetic and copies ran while one was open for 11% -> 0% of each run, Pallas kernels for 0% -> 0%
where the time goes in v1:
time: 231 us; the launch traced here: 230 us
  Pallas kernels  210 us (91%)
  other arithmetic  10.9 us (5%)
  local copies, waits for them, and re-layouts  8.59 us (4%)
    pallas_call x1, Pallas kernels, body(): pl.pallas_call(layer_kernel, out_shape=(jax.ShapeDtypeStruct((R, D), bf16...  210 us
    convert_element_type x5, other arithmetic, body(): grads = tuple((g.astype(f32) for g in grads))  9.19 us

profile of v1, /device:TPU:0, one launch (start us, length us, event | category | flops | bytes accessed | tf_op | source)
XLA Modules:
  0.0 230.4 jit_solution(12452752926162378025)
XLA Ops:
  0.6 0.7 dynamic-slice_compare_fusion
  1.4 1.3 reshape.130.again_ref
  2.6 1.3 reshape.132.gbias_ref
  3.9 1.3 reshape.131.fgain_ref
  5.1 0.1 broadcast_compare_fusion
  5.2 0.1 and_select_fusion.1
  5.4 0.8 pad_maximum_fusion.bias_ref
  6.2 210.2 %shard_map.220 = (bf16[512,768]{1,0:T(8,128)(2,1)}, bf16[512,768]{1,0:T(8,128)(2,1)}, bf16[2,2,768,768]{3,2,1,0:T(8,128)(2,1)}, bf16[4,2,96,768]{3,2,1,0:T(8,128)(2,1)}, f32[8,768]{1,0:T(8,128)}) custom-call(bf16[512,768]{1,0:T(8,128)(2,1)} %x_ref.1, bf16[512,768]{1,0:T(8,128)(2,1)} %og_ref.1, f32[2,4,128,128]{3,2,1,0:T(8,128)} %pad_maximum_fusion.bias_ref, ...), custom_call_target="tpu_custom_call" | custom-call | tf_op jit(solution)/shard_map/pallas_call | solution.py:772
  216.4 1.5 slice_reduce_fusion
  217.9 0.0 copy-start
  217.9 2.3 bitcast_convert_fusion.3
  220.2 1.5 fusion.1
  221.7 0.0 copy-done
  221.7 2.5 %bitcast_convert_fusion = (f32[768,768]{1,0:T(8,128)}, f32[768,768]{1,0:T(8,128)}) fusion(bf16[2,2,768,768]{3,2,1,0:T(8,128)(2,1)S(1)} %copy-done), kind=kLoop, calls=%fused_computation | loop fusion | flops 1179648 | bytes 7077888 | tf_op jit(solution)/shard_map/convert_element_type | solution.py:795
  224.3 0.0 copy-start.1
  224.3 1.4 convert.7
  225.6 1.4 convert.8
  227.0 0.0 copy-done.1
  227.0 0.0 copy-start.3
  227.0 0.0 copy-start.2
  227.0 1.7 bitcast_convert_fusion.2
  228.6 0.0 copy-done.3
  228.6 0.9 copy.27
  229.5 0.0 copy-done.2
  229.5 0.9 copy.28
  (1 shorter events, 0.0 us)
Async XLA Ops:
  217.9 3.8 %copy-start = (bf16[2,2,768,768]{3,2,1,0:T(8,128)(2,1)S(1)}, bf16[2,2,768,768]{3,2,1,0:T(8,128)(2,1)}, u32[]{:S(2)}) copy-start(bf16[2,2,768,768]{3,2,1,0:T(8,128)(2,1)} %get-tuple-element.20) | copy-start | bytes 14155780
  224.3 2.7 %copy-start.1 = (bf16[4,2,96,768]{3,2,1,0:T(8,128)(2,1)S(1)}, bf16[4,2,96,768]{3,2,1,0:T(8,128)(2,1)}, u32[]{:S(2)}) copy-start(bf16[4,2,96,768]{3,2,1,0:T(8,128)(2,1)} %get-tuple-element.21) | copy-start | bytes 3538948
  227.0 1.7 copy-start.3
  227.0 2.5 %copy-start.2 = (bf16[512,768]{1,0:T(8,128)(2,1)S(1)}, bf16[512,768]{1,0:T(8,128)(2,1)}, u32[]{:S(2)}) copy-start(bf16[512,768]{1,0:T(8,128)(2,1)} %get-tuple-element.48) | copy-start | bytes 2359300

commit v2 on v1

--- a/solution.py
+++ b/solution.py
@@ -18,6 +18,45 @@
 bf16 = jnp.bfloat16
 MESH = pl.DeviceIdType.MESH
 
+AFTER = {
+    "A0p1": (("zw", 0, 1), ("ag1", 0), ("zw", 0, 2),),
+    "A0p2": (("ag2", 0), ("zw", 0, 3), ("ag1", 1), ("ag3", 0), ("zs", 1),),
+    "A0p3": (("ag1", 2),),
+    "A0s": (("ag2", 1),),
+    "gate": (("ag2", 2),),
+    "A1p0": (("zw", 1, 1),),
+    "A1p1": (("zw", 1, 2), ("ag1", 3),),
+    "A1p3": (("ag3", 1),),
+    "A2q": (("zw", 1, 3), ("ag1", 4),),
+    "A2p0": (("ag3", 2),),
+    "A2s": (("ag2", 3),),
+    "A3p3": (("ag1", 5), ("ag2", 4),),
+    "F0a": (("ag3", 3),),
+    "F1a": (("rs0", 0), ("ag2", 5),),
+    "F1b": (("ag3", 4),),
+    "F1c": (("rs0", 1), ("rs1", 0),),
+    "F2a": (("rs1", 1), ("ag3", 5),),
+    "F3a": (("rs0", 2),),
+    "F3c": (("rs0", 3), ("rs1", 2),),
+    "mid2": (("rs1", 3),),
+    "ggrad": (("rs2", 0), ("rs2", 2), ("g", 0), ("rs0", 4),),
+    "B0p3": (("rs1", 4),),
+    "B1o": (("rs2", 3),),
+    "B1p0": (("rs3", 0), ("rs0", 5),),
+    "B1p2": (("rs3", 2), ("rs1", 5),),
+    "B1p3": (("rs2", 1),),
+    "B2o": (("rs3", 3), ("rs0", 6),),
+    "B2p0": (("rs2", 4), ("zza", 0, 2),),
+    "B2p2": (("rs3", 1), ("rs1", 6),),
+    "B2g": (("zza", 0, 3), ("g", 1), ("rs0", 7), ("rs2", 5),),
+    "B2h": (("rs1", 7), ("rs3", 4),),
+    "B3p1": (("rs3", 5), ("g", 2), ("rs2", 6),),
+    "B3p3": (("fin0", 0),),
+    "B3g": (("rs0", 8), ("zza", 1, 3), ("rs2", 7), ("g", 3), ("rs3", 6), ("zza", 2, 3), ("rs1", 8), ("fin1", 0), ("zza", 1, 2),),
+    "B3h": (("g", 4),),
+    "tail": (("g", 5), ("zza", 2, 2), ("rs3", 7), ("rs2", 8), ("v", 0), ("fin2", 0), ("v", 1), ("fin0", 1), ("g", 6), ("rs3", 8), ("fin0", 2), ("v", 2), ("fin1", 1), ("fin1", 2), ("v", 3), ("v", 4), ("fin3", 0), ("fin2", 1), ("g", 7), ("fin2", 2), ("g", 8), ("fin3", 1), ("fin3", 2),),
+}
+
 
 def mm(lhs, rhs, form):
     dims = {"nn": ((1,), (0,)), "nt": ((1,), (1,)), "tn": ((0,), (0,))}[form]
@@ -37,17 +76,21 @@
 
 
 def layer_kernel(
-    x_ref, og_ref, bias_ref, again_ref, fgain_ref, gate_ref, gbias_ref,
+    x_hbm, og_hbm, gate_hbm, marks_ref, again_ref, fgain_ref, gbias_ref,
     sq_ref, cq_ref, so_ref, co_ref, up_ref, dn_ref,
-    out_ref, tg_ref, fin, gout, vec_ref,
-    buf, crecv, p1a, p1b, p2a, p2b, zrv, gg, gcr, gxr, gyr, gzr, vs, vr, vz,
-    h, qkv, o, lse, sc, aa, mid, h2, acc, gh, eb, wb, gz,
-    loc, az_s, az_r, a1_s, a1_r, a2_s, a2_r, ac_s, ac_r,
-    rc_s, rc_r, r1_s, r1_r, r2_s, r2_r, rz_s, rz_r,
+    out_hbm, tg_hbm, fin, gout, vec_ref,
+    buf, crecv, p1a, p1b, p2a, p2b, cr_o, p1a_o, p1b_o, p2a_o, p2b_o,
+    z_f, z_o, z_q, e_f, e_o, e_q, gg, gcr, gxr, gyr, gzr, vs, vr, vz,
+    og_ref, bias_ref, h, qkv, o, lse, sc, aa, mid, h2, acc, gh, eb, wb,
+    io, loc, az_s, az_r, a1_s, a1_r, a2_s, a2_r, ac_s, ac_r,
+    rc_s, rc_r, r1_s, r1_r, r2_s, r2_r, rz_s, rz_r, re_r,
     f1_s, f1_r, f2_s, f2_r, fc_s, fc_r, fl,
     g_s, g_r, gz_s, gz_r, ga_s, ga_r, gl, v_s, v_r, vz_s, vz_r,
 ):
-    R, D = x_ref.shape
+    R, D = x_hbm.shape
+    gate_ref = buf.at[2, 0, 0]
+    x_ref = eb
+    gz = og_ref
     CH = buf.shape[3]
     XH, YH = CH // 2, D // 2
     AR = XH // 2
@@ -88,6 +131,11 @@
     for dev in partners:
         pl.semaphore_signal(bar, inc=1, device_id=dev, device_id_type=MESH)
 
+    ins = [
+        pltpu.make_async_copy(src, dst, io.at[i])
+        for i, (src, dst) in enumerate(((x_hbm, x_ref), (gate_hbm, gate_ref), (og_hbm, og_ref)))
+    ]
+    ins[0].start()
     local = []
     for i, (src, g, cc, r0) in enumerate(
         (
@@ -98,6 +146,8 @@
         cp = pltpu.make_async_copy(src, buf.at[g, cc, z, pl.ds(r0, src.shape[0]), :], loc.at[i])
         cp.start()
         local.append(cp)
+    ins[1].start()
+    ins[2].start()
 
     def wpart(g, cc, zz, r0, nr, c0, nc):
         return buf.at[g, cc, zz, blk(r0, nr, 16), blk(c0, nc, 128)]
@@ -159,40 +209,43 @@
             remote(theirs, theirs, ac_s.at[g, j], ac_r.at[g, j], dev_c),
         )
 
-    def pump_ag(t):
-        @pl.when(t < 6)
+    def ag_forward(g, j):
+        @pl.when(ismid == 1)
         def _():
-            g, j = t // 3, t % 3 + 1
             z_copy(g, zof(j), 1, 0, j).wait_recv()
-
-            @pl.when(ismid == 1)
-            def _():
-                is1 = 1 - j // 2
-                z_copy(g, zof(j), 2 * is1 + 1 - is1, j + 1, 3 * is1 + j * (1 - is1)).start()
-
-            for cp in ag_p1(g, j)[0]:
-                cp.start()
-
-        @pl.when((t >= 1) & (t < 7))
+            if j == 1:
+                z_copy(g, zof(1), 2, 2, 3).start()
+            else:
+                z_copy(g, zof(j), 1, j + 1, j).start()
+
+    def ag_1(t):
+        g, j = t // 3, t % 3 + 1
+
+        @pl.when(ismid == 0)
         def _():
-            g, j = (t - 1) // 3, (t - 1) % 3 + 1
-            outs, ins = ag_p1(g, j)
-            for cp in ins:
-                cp.wait_recv()
-            for cp in ag_p2(g, j)[0]:
-                cp.start()
-            for cp in outs:
-                cp.wait_send()
-
-        @pl.when((t >= 2) & (t < 8))
-        def _():
-            g, j = (t - 2) // 3, (t - 2) % 3 + 1
-            outs, ins = ag_p2(g, j)
-            for cp in ins:
-                cp.wait_recv()
-            ag_c(g, j)[0].start()
-            for cp in outs:
-                cp.wait_send()
+            z_copy(g, zof(j), 1, 0, j).wait_recv()
+
+        for cp in ag_p1(g, j)[0]:
+            cp.start()
+
+    def ag_2(t):
+        g, j = t // 3, t % 3 + 1
+        outs, arrivals = ag_p1(g, j)
+        for cp in arrivals:
+            cp.wait_recv()
+        for cp in ag_p2(g, j)[0]:
+            cp.start()
+        for cp in outs:
+            cp.wait_send()
+
+    def ag_3(t):
+        g, j = t // 3, t % 3 + 1
+        outs, arrivals = ag_p2(g, j)
+        for cp in arrivals:
+            cp.wait_recv()
+        ag_c(g, j)[0].start()
+        for cp in outs:
+            cp.wait_send()
 
     def ag_done(g, j):
         mine, theirs = ag_c(g, j)
@@ -200,7 +253,7 @@
         mine.wait_send()
 
     def add_rows(dst, dst_idx, r0, nr, c0, nc, src, src_idx):
-        step = 64 if nr % 64 == 0 else 48
+        step = next(n for n in (64, 48) if nr % n == 0)
 
         @pl.loop(0, nr // step)
         def _(i):
@@ -210,164 +263,205 @@
             t = src[(*src_idx, blk(i * step, step, 16), slice(None))].astype(f32)
             dst[(*dst_idx, rows, cols)] = (d + t).astype(bf16)
 
-    def rs_c(n):
-        return remote(buf.at[2 - n // 4, 1 - c, n % 4], crecv.at[n % 4], rc_s.at[n], rc_r.at[n], dev_c)
-
-    def rs_p1(n):
-        b, k = 2 - n // 4, n % 4
-        cps = [remote(buf.at[b, c, k, blk(XH * (1 - x), AR, 16), :], p1a.at[k], r1_s.at[n, 0], r1_r.at[n, 0], dev_x)]
+    def single(b, nr, ha, kq, slot, sem):
+        def reg(cc, r0, n, c0, w):
+            return buf.at[b, cc, kq, blk(r0, n, 16), blk(c0, w, 128)]
+
+        def add(r0, n, c0, w, src, idx):
+            add_rows(buf, (b, c, kq), r0, n, c0, w, src, idx)
+
+        return dict(
+            reg=reg, add=add, nr=nr, ha=ha, sem=sem,
+            cr=(crecv, (slot,), pl.ds(0, nr)), a1=(p1a, (slot,), pl.ds(0, ha)),
+            b1=[(p1b, (slot, xx), pl.ds(0, ha)) for xx in range(2)],
+            a2=(p2a, (slot,), pl.ds(0, ha)), b2=(p2b, (slot,), pl.ds(0, ha)),
+        )
+
+    def k_ffn(k):
+        return single(2, CH, AR, k, k, k)
+
+    def k_qkv(i):
+        return single(1, QR, QR // 4, 3 - i, i, 5 + i)
+
+    def k_out():
+        def reg(cc, r0, n, c0, w):
+            return buf.at[1, cc, :, blk(QR + r0, n, 16), blk(c0, w, 128)]
+
+        def add(r0, n, c0, w, src, idx):
+            for q in range(4):
+                add_rows(buf, (1, c, q), QR + r0, n, c0, w, src, (*idx, q))
+
+        every = slice(None)
+        return dict(
+            reg=reg, add=add, nr=F, ha=F // 4, sem=4,
+            cr=(cr_o, (), every), a1=(p1a_o, (), every), b1=[(p1b_o, (xx,), every) for xx in range(2)],
+            a2=(p2a_o, (), every), b2=(p2b_o, (), every),
+        )
+
+    def land(part):
+        ref, idx, rows = part
+        return ref.at[(*idx, rows)]
+
+    def rs_c(kd):
+        n = kd["sem"]
+        return remote(kd["reg"](1 - c, 0, kd["nr"], 0, D), land(kd["cr"]), rc_s.at[n], rc_r.at[n], dev_c)
+
+    def rs_p1(kd):
+        n, half, ha, reg = kd["sem"], kd["nr"] // 2, kd["ha"], kd["reg"]
+        cps = [remote(reg(c, half * (1 - x), ha, 0, D), land(kd["a1"]), r1_s.at[n, 0], r1_r.at[n, 0], dev_x)]
         for xx in range(2):
-            cps.append(
-                remote(
-                    buf.at[b, c, k, pl.ds(XH * xx + AR, AR), blk(YH * (1 - y), YH, 128)],
-                    p1b.at[k, xx], r1_s.at[n, 1 + xx], r1_r.at[n, 1 + xx], dev_y,
-                )
-            )
+            src = reg(c, half * xx + ha, ha, YH * (1 - y), YH)
+            cps.append(remote(src, land(kd["b1"][xx]), r1_s.at[n, 1 + xx], r1_r.at[n, 1 + xx], dev_y))
         return cps
 
-    def rs_p2(n):
-        b, k = 2 - n // 4, n % 4
+    def rs_p2(kd):
+        n, half, ha, reg = kd["sem"], kd["nr"] // 2, kd["ha"], kd["reg"]
+        return [
+            remote(reg(c, half * x, ha, YH * (1 - y), YH), land(kd["a2"]), r2_s.at[n, 0], r2_r.at[n, 0], dev_y),
+            remote(
+                reg(c, half * (1 - x) + ha, ha, YH * y, YH), land(kd["b2"]), r2_s.at[n, 1], r2_r.at[n, 1], dev_x
+            ),
+        ]
+
+    def rs_0(kd):
+        rs_c(kd).start()
+
+    def rs_1(kd, between=None):
+        cp = rs_c(kd)
+        cp.wait_recv()
+        kd["add"](0, kd["nr"], 0, D, kd["cr"][0], kd["cr"][1])
+        if between is not None:
+            between()
+        for q in rs_p1(kd):
+            q.start()
+        cp.wait_send()
+
+    def rs_2(kd):
+        half, ha = kd["nr"] // 2, kd["ha"]
+        cps = rs_p1(kd)
+        for q in cps:
+            q.wait_recv()
+        kd["add"](half * x, ha, 0, D, kd["a1"][0], kd["a1"][1])
+        for xx in range(2):
+            kd["add"](half * xx + ha, ha, YH * y, YH, kd["b1"][xx][0], kd["b1"][xx][1])
+        for q in rs_p2(kd):
+            q.start()
+        for q in cps:
+            q.wait_send()
+
+    def rs_3(kd, after=None):
+        half, ha = kd["nr"] // 2, kd["ha"]
+        cps = rs_p2(kd)
+        for q in cps:
+            q.wait_recv()
+        kd["add"](half * x, ha, YH * y, YH, kd["a2"][0], kd["a2"][1])
+        kd["add"](half * x + ha, ha, YH * y, YH, kd["b2"][0], kd["b2"][1])
+        if after is not None:
+            after()
+        for q in cps:
+            q.wait_send()
+
+    groups = ((2, 0, XH, z_f, e_f), (1, QR, F // 2, z_o, e_o), (1, 0, QR // 2, z_q, e_q))
+
+    def z_part(gi, k):
+        b, r0, half = groups[gi][:3]
+        return buf.at[b, c, k, blk(r0 + half * x, half, 16), blk(YH * y, YH, 128)]
+
+    def z_out(gi, k):
+        return remote(z_part(gi, k), groups[gi][3].at[0 if k == 1 else 1], rz_s.at[gi, k], rz_r.at[gi, 0 if k == 1 else 1], (dp, zof(k)))
+
+    def z_hop(gi, k):
+        return remote(z_part(gi, k), groups[gi][4].at[k - 2], rz_s.at[gi, k], re_r.at[gi, k - 2], (dp, zof(1)))
+
+    def z_start(gi, k):
+        if k == 1:
+            z_out(gi, 1).start()
+        if k > 1:
+
+            @pl.when(ismid == 0)
+            def _():
+                z_hop(gi, k).start()
+
+    def z_join(gi, k):
+        b, r0, half, _to, mid_buf = groups[gi]
+
+        @pl.when(ismid == 1)
+        def _():
+            z_hop(gi, k).wait_recv()
+            add_rows(buf, (b, c, k), r0 + half * x, half, YH * y, YH, mid_buf, (k - 2,))
+            z_out(gi, k).start()
+
+    def fin_part(gi, r, n, c0, w):
+        r0 = groups[gi][1]
+        return fin.at[0 if gi == 0 else 1, c, blk(r0 + r, n, 16), blk(c0, w, 128)]
+
+    def own_part(gi, r, n):
+        b, r0 = groups[gi][:2]
+        return buf.at[b, c, 0, blk(r0 + r, n, 16), blk(YH * y, YH, 128)]
+
+    def fin_p1(gi):
+        half = groups[gi][2]
+        q = half // 2
         return [
             remote(
-                buf.at[b, c, k, blk(XH * x, AR, 16), blk(YH * (1 - y), YH, 128)],
-                p2a.at[k], r2_s.at[n, 0], r2_r.at[n, 0], dev_y,
-            ),
-            remote(
-                buf.at[b, c, k, blk(XH * (1 - x) + AR, AR, 16), blk(YH * y, YH, 128)],
-                p2b.at[k], r2_s.at[n, 1], r2_r.at[n, 1], dev_x,
-            ),
+                own_part(gi, half * x + q * i, q), fin_part(gi, half * x + q * i, q, YH * y, YH),
+                f1_s.at[gi, i], f1_r.at[gi, i], dev,
+            )
+            for i, dev in enumerate((dev_x, dev_y))
         ]
 
-    def rs_z(n, rslot):
-        b, k, g = 2 - n // 4, n % 4, n // 4
-        return remote(
-            buf.at[b, c, k, blk(XH * x, XH, 16), blk(YH * y, YH, 128)],
-            zrv.at[g, rslot - 1], rz_s.at[n], rz_r.at[g, rslot], (dp, zof(k)),
+    def fin_local(gi):
+        half = groups[gi][2]
+        return pltpu.make_async_copy(
+            own_part(gi, half * x, half), fin_part(gi, half * x, half, YH * y, YH), fl.at[gi]
         )
 
-    def pump_rs(t):
-        def chunk(v):
-            return v - v // 5
-
-        def has(v):
-            return (v >= 0) & (v < 9) & (v != 4)
-
-        @pl.when(has(t))
-        def _():
-            rs_c(chunk(t)).start()
-
-        @pl.when(has(t - 1))
-        def _():
-            n = chunk(t - 1)
-            cp = rs_c(n)
-            cp.wait_recv()
-            add_rows(buf, (2 - n // 4, c, n % 4), 0, CH, 0, D, crecv, (n % 4,))
-            for q in rs_p1(n):
-                q.start()
-            cp.wait_send()
-
-        @pl.when(has(t - 2))
-        def _():
-            n = chunk(t - 2)
-            idx = (2 - n // 4, c, n % 4)
-            cps = rs_p1(n)
-            for q in cps:
-                q.wait_recv()
-            add_rows(buf, idx, XH * x, AR, 0, D, p1a, (n % 4,))
-            for xx in range(2):
-                add_rows(buf, idx, XH * xx + AR, AR, YH * y, YH, p1b, (n % 4, xx))
-            for q in rs_p2(n):
-                q.start()
-            for q in cps:
-                q.wait_send()
-
-        @pl.when(has(t - 3))
-        def _():
-            n = chunk(t - 3)
-            idx = (2 - n // 4, c, n % 4)
-            cps = rs_p2(n)
-            for q in cps:
-                q.wait_recv()
-            add_rows(buf, idx, XH * x, AR, YH * y, YH, p2a, (n % 4,))
-            add_rows(buf, idx, XH * x + AR, AR, YH * y, YH, p2b, (n % 4,))
-
-            @pl.when(n % 4 != 0)
-            def _():
-                rs_z(n, seen_as(n % 4)).start()
-
-            for q in cps:
-                q.wait_send()
-
-    def fin_part(g, r0, nr, c0, nc):
-        return fin.at[g, c, blk(r0, nr, 16), blk(c0, nc, 128)]
-
-    def fin_p1(g):
-        b = 2 - g
-        return [
-            remote(
-                buf.at[b, c, 0, blk(XH * x, AR, 16), blk(YH * y, YH, 128)],
-                fin_part(g, XH * x, AR, YH * y, YH), f1_s.at[g, 0], f1_r.at[g, 0], dev_x,
-            ),
-            remote(
-                buf.at[b, c, 0, blk(XH * x + AR, AR, 16), blk(YH * y, YH, 128)],
-                fin_part(g, XH * x + AR, AR, YH * y, YH), f1_s.at[g, 1], f1_r.at[g, 1], dev_y,
-            ),
-        ]
-
-    def fin_local(g):
-        return pltpu.make_async_copy(
-            buf.at[2 - g, c, 0, blk(XH * x, XH, 16), blk(YH * y, YH, 128)],
-            fin_part(g, XH * x, XH, YH * y, YH), fl.at[g],
-        )
-
-    def fin_p2(g):
+    def fin_p2(gi):
+        half = groups[gi][2]
+        q = half // 2
         cps = []
         for xx in range(2):
-            ref = fin_part(g, XH * xx, AR, YH * y, YH)
-            cps.append(remote(ref, ref, f2_s.at[g, xx], f2_r.at[g, xx], dev_y))
-        ref = fin_part(g, XH * x + AR, AR, 0, D)
-        cps.append(remote(ref, ref, f2_s.at[g, 2], f2_r.at[g, 2], dev_x))
+            ref = fin_part(gi, half * xx, q, YH * y, YH)
+            cps.append(remote(ref, ref, f2_s.at[gi, xx], f2_r.at[gi, xx], dev_y))
+        ref = fin_part(gi, half * x + q, q, 0, D)
+        cps.append(remote(ref, ref, f2_s.at[gi, 2], f2_r.at[gi, 2], dev_x))
         return cps
 
-    def fin_c(g):
-        return remote(fin.at[g, c], fin.at[g, c], fc_s.at[g], fc_r.at[g], dev_c)
-
-    def fin_step0(g):
-        b = 2 - g
-        for slot in range(1, 4):
-            rs_z(4 * g + slot, slot).wait_recv()
-        for i in range(XH // 64):
-            rows = blk(XH * x + 64 * i, 64, 16)
-            cols = blk(YH * y, YH, 128)
-            t = buf[b, c, 0, rows, cols].astype(f32)
-            for slot in range(3):
-                t = t + zrv[g, slot, pl.ds(64 * i, 64), :].astype(f32)
-            buf[b, c, 0, rows, cols] = t.astype(bf16)
-        fin_local(g).start()
-        for q in fin_p1(g):
+    def fin_c(gi):
+        ref = fin_part(gi, 0, 2 * groups[gi][2], 0, D)
+        return remote(ref, ref, fc_s.at[gi], fc_r.at[gi], dev_c)
+
+    def fin_0(gi):
+        b, r0, half, part, _mid = groups[gi]
+        for k in (1, 2):
+            z_out(gi, k).wait_recv()
+        for slot in range(2):
+            add_rows(buf, (b, c, 0), r0 + half * x, half, YH * y, YH, part, (slot,))
+        for q in fin_p1(gi):
             q.start()
-        for slot in range(1, 4):
-            rs_z(4 * g + slot, slot).wait_send()
-
-    def fin_step1(g):
-        for q in fin_p1(g):
+        fin_local(gi).start()
+        for k in (1, 2, 3):
+            z_out(gi, k).wait_send()
+
+    def fin_1(gi):
+        for q in fin_p1(gi):
             q.wait_recv()
-        fin_local(g).wait()
-        for q in fin_p2(g):
+        fin_local(gi).wait()
+        for q in fin_p2(gi):
             q.start()
-        for q in fin_p1(g):
+        for q in fin_p1(gi):
             q.wait_send()
 
-    def fin_step2(g):
-        for q in fin_p2(g):
+    def fin_2(gi):
+        for q in fin_p2(gi):
             q.wait_recv()
-        fin_c(g).start()
-        for q in fin_p2(g):
+        fin_c(gi).start()
+        for q in fin_p2(gi):
             q.wait_send()
 
-    def fin_step3(g):
-        fin_c(g).wait_recv()
-        fin_c(g).wait_send()
+    def fin_3(gi):
+        fin_c(gi).wait_recv()
+        fin_c(gi).wait_send()
 
     def g_copy(i):
         xs, xo = blk(GX * x, GX, 16), blk(GX * (1 - x), GX, 16)
@@ -477,15 +571,59 @@
             for slot in range(1, 4):
                 v_z(slot, z, slot).wait_send()
 
+    def kind(n):
+        return k_ffn(n) if n < 4 else k_out() if n == 4 else k_qkv(n - 5)
+
+    def third(n):
+        if n < 4:
+            rs_3(kind(n), lambda: z_start(0, n))
+        elif n == 4:
+            rs_3(kind(n), lambda: [z_start(1, q) for q in range(1, 4)])
+        else:
+            rs_3(kind(n), lambda: z_start(2, 8 - n))
+
+    events = {
+        "zs": ag_zsend, "zw": ag_forward, "ag1": ag_1, "ag2": ag_2, "ag3": ag_3,
+        "rs0": lambda n: rs_0(kind(n)), "rs1": lambda n: rs_1(kind(n)), "rs2": lambda n: rs_2(kind(n)), "rs3": third,
+        "zza": z_join, "g": g_step, "v": v_step, "fin0": fin_0, "fin1": fin_1, "fin2": fin_2, "fin3": fin_3,
+    }
+
+    def after(name, k=None, p=None):
+        if k is None:
+            for ev in AFTER.get(name, ()):
+                events[ev[0]](*ev[1:])
+            return
+        for kk in range(4):
+            for pp in range(1 if p is None else 4):
+                found = AFTER.get(name[0] + str(kk) + name[1:] + ("" if p is None else str(pp)), ())
+                if found:
+
+                    @pl.when((k == kk) if p is None else (k == kk) & (p == pp))
+                    def _():
+                        for ev in found:
+                            events[ev[0]](*ev[1:])
+
+    TR = 64
+    again = again_ref[...].astype(f32).reshape(1, D)
+    fgain = fgain_ref[...].astype(f32).reshape(1, D)
+    gbias = gbias_ref[...].astype(f32).reshape(1, D)
+
     pl.semaphore_wait(bar, 6)
     for cp in local[:4]:
         cp.wait()
     ag_zsend(0)
 
-    TR = 64
-    again = again_ref[...].astype(f32)
-    fgain = fgain_ref[...].astype(f32)
-    gbias = gbias_ref[...].astype(f32)
+    key_id = lax.broadcasted_iota(jnp.int32, (SLOTS, SLOTS), 0)
+    query_id = lax.broadcasted_iota(jnp.int32, (SLOTS, SLOTS), 1)
+    key_kind = jnp.where(key_id < LANG, 1, 0)
+    query_kind = jnp.where(query_id < LANG, 1, 0)
+    for p in range(pages):
+        row = marks_ref[pl.ds(pages * z + p, 1), :]
+        real = jnp.broadcast_to(jnp.where(row > 0, 0.0, NEG), (SLOTS, SLOTS)).T
+        bias_ref[0, p] = jnp.where(key_kind == query_kind, real, NEG).astype(bf16)
+        bias_ref[1, p] = jnp.where(key_kind == query_kind, NEG, real).astype(bf16)
+
+    ins[0].wait()
 
     @pl.loop(0, R // TR)
     def _(i):
@@ -497,17 +635,9 @@
         gh[rows, :] = jnp.zeros((TR, D), f32)
 
     vs[...] = jnp.zeros_like(vs)
-    for cp in local[4:]:
+    for cp in local[4:] + ins[1:]:
         cp.wait()
-    ag_zsend(1)
-    pump_ag(0)
-
-    @pl.loop(0, R // 128)
-    def _(i):
-        rows = blk(i * 128, 128, 16)
-        aa[rows, :] = jax.nn.sigmoid(mm(h[rows, :], gate_ref[...], "nn") + gbias)
-
-    pump_ag(1)
+    after("norm")
 
     @pl.loop(0, 4)
     def _(k):
@@ -519,6 +649,7 @@
 
         for at in range(2):
             qkv[at, k] = mm(buf[0, at, zz, 0:QR, :], h[...], "nt").astype(bf16)
+        after("Aq", k)
 
         @pl.loop(0, pages)
         def _(p):
@@ -528,17 +659,31 @@
                     qt = qkv[at, k, HEAD * hh : HEAD * (hh + 1), cols]
                     kt = qkv[at, k, F + HEAD * hh : F + HEAD * (hh + 1), cols]
                     vt = qkv[at, k, 2 * F + HEAD * hh : 2 * F + HEAD * (hh + 1), cols]
-                    st = mm(kt, qt, "tn") * HEAD ** (-0.5) + bias_ref[at, p]
+                    st = mm(kt, qt, "tn") * HEAD ** (-0.5) + bias_ref[at, p].astype(f32)
                     top = jnp.max(st, axis=0, keepdims=True)
                     ex = jnp.exp(st - top)
                     tot = jnp.sum(ex, axis=0, keepdims=True)
                     pt = (ex * (1.0 / tot)).astype(bf16)
                     lse[at, k, hh : hh + 1, cols] = top + jnp.log(tot)
                     o[at, k, HEAD * hh : HEAD * (hh + 1), cols] = mm(vt, pt, "nn").astype(bf16)
-
-        for at, dst in ((0, sc), (1, mid)):
-            dst[...] += mm(o[at, k], buf[0, at, zz, QR:CH, :], "tn")
-        pump_ag(k + 2)
+            after("Ap", k, p)
+
+        @pl.loop(0, pages)
+        def _(p):
+            cols = blk(p * SLOTS, SLOTS, 128)
+            for at, dst in ((0, sc), (1, mid)):
+                dst[cols, :] += mm(o[at, k, :, cols], buf[0, at, zz, QR:CH, :], "tn")
+
+        after("As", k)
+
+        @pl.when(k == 0)
+        def _():
+            @pl.loop(0, R // 128)
+            def _(i):
+                rows = blk(i * 128, 128, 16)
+                aa[rows, :] = jax.nn.sigmoid(mm(h[rows, :], gate_ref[...], "nn") + gbias)
+
+            after("gate")
 
     ag_zsend_wait(0)
 
@@ -554,6 +699,8 @@
         u, _inv = standardize(mv)
         h2[rows, :] = (u * fgain).astype(bf16)
 
+    after("join")
+
     @pl.loop(0, 4)
     def _(k):
         zz = zof(k)
@@ -576,23 +723,23 @@
             dg = half + 0.5 * w * (1.0 - th * th) * (GC * (1.0 + 3.0 * GK * w2))
             wb[rows, :] = (dg * ge).astype(bf16)
 
+        after("Fa", k)
+
         @pl.loop(0, R // MT)
         def _(i):
             rows = blk(i * MT, MT, 16)
             acc[rows, :] += mm(eb[rows, :], buf[1, 1, zz], "nn")
             gh[rows, :] += mm(wb[rows, :], buf[1, 0, zz], "nt")
 
+        after("Fb", k)
+
         @pl.loop(0, CH // 256)
         def _(i):
             cols = blk(i * 256, 256, 128)
             buf[2, 1, k, blk(i * 256, 256, 16), :] = mm(eb[:, cols], og_ref[...], "tn").astype(bf16)
             buf[2, 0, k, blk(i * 256, 256, 16), :] = mm(h2[:, cols], wb[...], "tn").astype(bf16)
 
-        pump_rs(k)
-
-        @pl.when(k < 2)
-        def _():
-            pump_ag(k + 6)
+        after("Fc", k)
 
     ag_zsend_wait(1)
 
@@ -602,8 +749,7 @@
     def mid_back(i, sums):
         gain_sum, bias_sum = sums
         rows = blk(i * TS, TS, 16)
-        ov = acc[rows, :]
-        out_ref[rows, :] = ov.astype(bf16)
+        h2[rows, :] = acc[rows, :].astype(bf16)
         u, inv = standardize(mid[rows, :])
         gy = gh[rows, :]
         gain_sum = gain_sum + jnp.sum(gy * u, axis=0, keepdims=True)
@@ -612,7 +758,6 @@
         m2 = jnp.mean(sy * u, axis=1, keepdims=True)
         gm = og_ref[rows, :].astype(f32) + inv * (sy - m1 - u * m2)
         acc[rows, :] = gm
-        gh[rows, :] = jnp.zeros((TS, D), f32)
         a = aa[rows, :]
         eb[rows, :] = (a * gm).astype(bf16)
         wb[rows, :] = ((1.0 - a) * gm).astype(bf16)
@@ -624,20 +769,38 @@
     gain_sum, bias_sum = lax.fori_loop(0, R // TS, mid_back, (zero_row, zero_row))
     vs[0, 1:2, :] = bias_sum
     vs[0, 2:3, :] = gain_sum
-    pump_rs(4)
-
+    out_copy = pltpu.make_async_copy(h2, out_hbm, io.at[3])
+    out_copy.start()
+    after("mid2")
+    gate_again = buf.at[2, 1 - c, 1]
+    gate_load = pltpu.make_async_copy(gate_hbm, gate_again, io.at[5])
+    gate_load.start()
+
+    for k in range(4):
+        for at, gref in ((0, eb), (1, wb)):
+            buf[1, at, k, QR:CH, :] = mm(o[at, k], gref[...], "nn").astype(bf16)
+    after("outmm")
     for i in range(4):
         t = mm(h[:, F * i : F * (i + 1)], gz[...], "tn").astype(bf16)
         gg[i, 0] = t[: F // 2]
         gg[i, 1] = t[F // 2 :]
-    g_step(0)
+    after("ggrad")
+
+    x_again = wb
+    x_load = pltpu.make_async_copy(x_hbm, x_again, io.at[6])
 
     @pl.loop(0, 4)
-    def _(k):
+    def _(i):
+        k = 3 - i
         zz = zof(k)
         for at, gref in ((0, eb), (1, wb)):
-            buf[1, at, k, QR:CH, :] = mm(o[at, k], gref[...], "nn").astype(bf16)
             o[at, k] = mm(buf[0, at, zz, QR:CH, :], gref[...], "nt").astype(bf16)
+
+        @pl.when(i == 3)
+        def _():
+            x_load.start()
+
+        after("Bo", i)
 
         @pl.loop(0, pages)
         def _(p):
@@ -651,7 +814,7 @@
                     kt = qkv[at, k, ks, cols]
                     vt = qkv[at, k, vsl, cols]
                     go = o[at, k, qs, cols]
-                    st = mm(kt, qt, "tn") * HEAD ** (-0.5) + bias_ref[at, p]
+                    st = mm(kt, qt, "tn") * HEAD ** (-0.5) + bias_ref[at, p].astype(f32)
                     pt = jnp.exp(st - lse[at, k, hh : hh + 1, cols])
                     gvt = mm(go, pt.astype(bf16), "nt")
                     gpt = mm(vt, go, "tn")
@@ -662,56 +825,100 @@
                     qkv[at, k, qs, cols] = gqt.astype(bf16)
                     qkv[at, k, ks, cols] = gkt.astype(bf16)
                     qkv[at, k, vsl, cols] = gvt.astype(bf16)
+            after("Bp", i, p)
 
         for at in range(2):
-            buf[1, at, k, 0:QR, :] = mm(qkv[at, k], h[...], "nn").astype(bf16)
-        pump_rs(5 + k)
-        for i in range(4):
-
-            @pl.when(k == i)
+            for q in range(3):
+                part = slice(F * q, F * (q + 1))
+                buf[1, at, k, part, :] = mm(qkv[at, k, part, :], h[...], "nn").astype(bf16)
+        after("Bg", i)
+
+        @pl.loop(0, pages)
+        def _(p):
+            cols = blk(p * SLOTS, SLOTS, 128)
+            t = mm(qkv[0, k, :, cols], buf[0, 0, zz, 0:QR, :], "tn") + mm(qkv[1, k, :, cols], buf[0, 1, zz, 0:QR, :], "tn")
+
+            @pl.when(i == 0)
             def _():
-                g_step(i + 1)
-
-        for at in range(2):
-            gh[...] += mm(qkv[at, k], buf[0, at, zz, 0:QR, :], "tn")
+                gh[cols, :] = t
+
+            @pl.when(i > 0)
+            def _():
+                gh[cols, :] += t
+
+        after("Bh", i)
+
+    gate_load.wait()
 
     @pl.loop(0, R // 128)
     def _(i):
         rows = blk(i * 128, 128, 16)
-        gh[rows, :] += mm(gz[rows, :], gate_ref[...], "nt")
+        gh[rows, :] += mm(gz[rows, :], gate_again[...], "nt")
 
     def first_back(i, gain_sum):
         rows = blk(i * TS, TS, 16)
-        u, inv = standardize(x_ref[rows, :].astype(f32))
+        u, inv = standardize(x_again[rows, :].astype(f32))
         gy = gh[rows, :]
         gain_sum = gain_sum + jnp.sum(gy * u, axis=0, keepdims=True)
         sy = gy * again
         m1 = jnp.mean(sy, axis=1, keepdims=True)
         m2 = jnp.mean(sy * u, axis=1, keepdims=True)
-        tg_ref[rows, :] = (acc[rows, :] + inv * (sy - m1 - u * m2)).astype(bf16)
+        eb[rows, :] = (acc[rows, :] + inv * (sy - m1 - u * m2)).astype(bf16)
         return gain_sum
 
+    x_load.wait()
     vs[0, 0:1, :] = lax.fori_loop(0, R // TS, first_back, zero_row)
-    v_step(0)
-    pump_rs(9)
-    g_step(5)
-    fin_step0(0)
-    v_step(1)
-    pump_rs(10)
-    g_step(6)
-    fin_step1(0)
-    v_step(2)
-    pump_rs(11)
-    g_step(7)
-    fin_step2(0)
-    v_step(3)
-    fin_step0(1)
-    g_step(8)
-    fin_step3(0)
-    v_step(4)
-    fin_step1(1)
-    fin_step2(1)
-    fin_step3(1)
+    tg_copy = pltpu.make_async_copy(eb, tg_hbm, io.at[4])
+    tg_copy.start()
+    after("tail")
+    out_copy.wait()
+    tg_copy.wait()
+
+
+def widen_kernel(
+    out_in, tg_in, fin, gout, vec_in,
+    out_o, tg_o, ag_o, sq_o, cq_o, so_o, co_o, gw_o, gb_o, fg_o, up_o, dn_o,
+    narrow, wide, whole, sem_in, sem_out, sem_pass,
+):
+    F = so_o.shape[0]
+    QR = 3 * F
+    passes = []
+    for i, (src, dst) in enumerate(((out_in, out_o), (tg_in, tg_o))):
+        load = pltpu.make_async_copy(src, whole.at[i], sem_pass.at[i])
+        passes.append((load, pltpu.make_async_copy(whole.at[i], dst, sem_pass.at[2 + i])))
+    parts = [(fin.at[0, 0], up_o), (fin.at[0, 1], dn_o), (gout, gw_o)]
+    for cc, (a, b) in enumerate(((sq_o, so_o), (cq_o, co_o))):
+        parts += [(fin.at[1, cc, pl.ds(0, QR)], a), (fin.at[1, cc, pl.ds(QR, F)], b)]
+    r0 = 0
+    jobs = []
+    for i, (src, dst) in enumerate(parts):
+        n = src.shape[0]
+        load = pltpu.make_async_copy(src, narrow.at[pl.ds(r0, n)], sem_in.at[i])
+        save = pltpu.make_async_copy(wide.at[pl.ds(r0, n)], dst, sem_out.at[i])
+        load.start()
+        jobs.append((r0, n, load, save))
+        r0 += n
+    for load, _ in passes:
+        load.start()
+    ag_o[...] = vec_in[0, :]
+    gb_o[...] = vec_in[1, :]
+    fg_o[...] = vec_in[2, :]
+    for load, save in passes:
+        load.wait()
+        save.start()
+    for r0, n, load, save in jobs:
+        load.wait()
+
+        @pl.loop(0, n // 64)
+        def _(i):
+            rows = blk(r0 + 64 * i, 64, 16)
+            wide[rows, :] = narrow[rows, :].astype(f32)
+
+        save.start()
+    for _, _, _, save in jobs:
+        save.wait()
+    for _, save in passes:
+        save.wait()
 
 
 def body(
@@ -723,16 +930,11 @@
     QR = 3 * F
     CH = QR + F
     pages = R // SLOTS
-    marks = lax.dynamic_slice_in_dim(region_mask, lax.axis_index("mp") * pages, pages, 0)
-    lang = jnp.arange(SLOTS) < LANG
-    same = lang[:, None] == lang[None, :]
-    real = (marks > 0)[:, :, None]
-    bias = jnp.stack([jnp.where(same[None] & real, 0.0, NEG), jnp.where(~same[None] & real, 0.0, NEG)]).astype(f32)
 
     vm = pl.BlockSpec(memory_space=pltpu.VMEM)
     hb = pl.BlockSpec(memory_space=pl.ANY)
     dma = pltpu.SemaphoreType.DMA
-    XH, YH, AR, GX = CH // 2, D // 2, CH // 4, D // 16
+    XH, YH, AR, GX, OR = CH // 2, D // 2, CH // 4, D // 16, F // 4
     scratch = [
         pltpu.VMEM((3, 2, 4, CH, D), bf16),
         pltpu.VMEM((4, CH, D), bf16),
@@ -740,7 +942,17 @@
         pltpu.VMEM((4, 2, AR, YH), bf16),
         pltpu.VMEM((4, AR, YH), bf16),
         pltpu.VMEM((4, AR, YH), bf16),
-        pltpu.VMEM((2, 3, XH, YH), bf16),
+        pltpu.VMEM((4, F, D), bf16),
+        pltpu.VMEM((4, OR, D), bf16),
+        pltpu.VMEM((2, 4, OR, YH), bf16),
+        pltpu.VMEM((4, OR, YH), bf16),
+        pltpu.VMEM((4, OR, YH), bf16),
+        pltpu.VMEM((2, XH, YH), bf16),
+        pltpu.VMEM((2, F // 2, YH), bf16),
+        pltpu.VMEM((2, QR // 2, YH), bf16),
+        pltpu.VMEM((2, XH, YH), bf16),
+        pltpu.VMEM((2, F // 2, YH), bf16),
+        pltpu.VMEM((2, QR // 2, YH), bf16),
         pltpu.VMEM((4, 2, 2 * GX, D), bf16),
         pltpu.VMEM((4, 2 * GX, D), bf16),
         pltpu.VMEM((4, GX, D), bf16),
@@ -749,6 +961,8 @@
         pltpu.VMEM((3, 8, D), f32),
         pltpu.VMEM((3, 8, D), f32),
         pltpu.VMEM((4, 8, D), f32),
+        pltpu.VMEM((R, D), bf16),
+        pltpu.VMEM((2, pages, SLOTS, SLOTS), bf16),
         pltpu.VMEM((R, D), bf16),
         pltpu.VMEM((2, 4, QR, R), bf16),
         pltpu.VMEM((2, 4, F, R), bf16),
@@ -761,15 +975,16 @@
         pltpu.VMEM((R, D), f32),
         pltpu.VMEM((R, D), bf16),
         pltpu.VMEM((R, D), bf16),
-        pltpu.VMEM((R, D), bf16),
+        dma((7,)),
         dma((6,)), dma((2, 5)), dma((2, 4)), dma((2, 4, 2)), dma((2, 4, 2)), dma((2, 4, 3)), dma((2, 4, 3)),
         dma((2, 4)), dma((2, 4)),
-        dma((8,)), dma((8,)), dma((8, 3)), dma((8, 3)), dma((8, 2)), dma((8, 2)), dma((8,)), dma((2, 4)),
-        dma((2, 2)), dma((2, 2)), dma((2, 3)), dma((2, 3)), dma((2,)), dma((2,)), dma((2,)),
+        dma((9,)), dma((9,)), dma((9, 3)), dma((9, 3)), dma((9, 2)), dma((9, 2)), dma((3, 4)), dma((3, 2)),
+        dma((3, 2)),
+        dma((3, 2)), dma((3, 2)), dma((3, 3)), dma((3, 3)), dma((3,)), dma((3,)), dma((3,)),
         dma((6,)), dma((6,)), dma((4,)), dma((4,)), dma((4,)), dma((4,)), dma((1,)),
         dma((3,)), dma((3,)), dma((4,)), dma((4,)),
     ]
-    out, tg, fin, gout, vec = pl.pallas_call(
+    mid_out = pl.pallas_call(
         layer_kernel,
         out_shape=(
             jax.ShapeDtypeStruct((R, D), bf16),
@@ -778,21 +993,36 @@
             jax.ShapeDtypeStruct((4, 2, 2 * GX, D), bf16),
             jax.ShapeDtypeStruct((8, D), f32),
         ),
-        in_specs=[vm] * 7 + [hb] * 6,
-        out_specs=(vm, vm, hb, hb, vm),
+        in_specs=[hb] * 3 + [vm] * 4 + [hb] * 6,
+        out_specs=(hb, hb, hb, hb, vm),
         scratch_shapes=scratch,
         compiler_params=pltpu.CompilerParams(
             collective_id=1, has_side_effects=True, vmem_limit_bytes=64 * 2**20 - 2**17
         ),
     )(
-        tokens, out_grad, bias, attn_gain.reshape(1, D), ffn_gain.reshape(1, D), gate_weight, gate_bias.reshape(1, D),
+        tokens, out_grad, gate_weight, region_mask, attn_gain, ffn_gain, gate_bias,
         self_qkv.reshape(QR, D), cross_qkv.reshape(QR, D), self_out, cross_out, up_weight, down_weight,
     )
-    grads = (
-        vec[0], fin[1, 0, :QR].reshape(3, F, D), fin[1, 1, :QR].reshape(3, F, D), fin[1, 0, QR:], fin[1, 1, QR:],
-        gout.reshape(D, D), vec[1], vec[2], fin[0, 0], fin[0, 1],
-    )
-    grads = tuple(g.astype(f32) for g in grads)
+    out, tg, fin, gout, vec = mid_out
+    total = 4 * CH + D
+    wide = lambda *shape: jax.ShapeDtypeStruct(shape, f32)
+    res = pl.pallas_call(
+        widen_kernel,
+        out_shape=(
+            jax.ShapeDtypeStruct((R, D), bf16), jax.ShapeDtypeStruct((R, D), bf16),
+            wide(D), wide(QR, D), wide(QR, D), wide(F, D), wide(F, D), wide(D, D), wide(D), wide(D),
+            wide(CH, D), wide(CH, D),
+        ),
+        in_specs=[hb] * 4 + [vm],
+        out_specs=(hb, hb, vm, hb, hb, hb, hb, hb, vm, vm, hb, hb),
+        scratch_shapes=[
+            pltpu.VMEM((total, D), bf16), pltpu.VMEM((total, D), f32), pltpu.VMEM((2, R, D), bf16),
+            dma((7,)), dma((7,)), dma((4,)),
+        ],
+        compiler_params=pltpu.CompilerParams(vmem_limit_bytes=60 * 2**20),
+    )(out, tg, fin, gout.reshape(D, D), vec)
+    out, tg, again, sq, cq, so, co, gw, gb, fg, up, dn = res
+    grads = (again, sq.reshape(3, F, D), cq.reshape(3, F, D), so, co, gw, gb, fg, up, dn)
     if outer > 1:
         first = (lax.axis_index("dp") % 8 == 0).astype(f32)
         grads = lax.psum(tuple(g * first for g in grads), "dp")

time: 231 us -> 200 us (0.87)
  Pallas kernels: 210 us -> 199 us
  other arithmetic: 10.9 us -> 0 us
  local copies, waits for them, and re-layouts: 8.59 us -> 0 us
    pallas_call x1, Pallas kernels: 210 us -> 190 us  [body(): pl.pallas_call(layer_kernel, out_shape=(jax.ShapeDtypeStruct((R, D), bf16...]
    pallas_call x0 -> x1, Pallas kernels: none -> 9.22 us  [body(): pl.pallas_call(widen_kernel, out_shape=(jax.ShapeDtypeStruct((R, D), bf16...]
    convert_element_type x5 -> x0, other arithmetic: 9.19 us -> none  [body(): grads = tuple((g.astype(f32) for g in grads))]
    reshape x3 -> x0, local copies, waits for them, and re-layouts: 3.79 us -> none  [the longest x1 1.26 us: body(): attn_gain.reshape(1, D)]
    slice x2 -> x0, local copies, waits for them, and re-layouts: 3.03 us -> none  [the longest x1 1.55 us: body(): fin[1, 1, :QR].reshape(3, F, D)]
where the time goes in v2:
time: 200 us
  Pallas kernels  199 us (100%)
    pallas_call x1, Pallas kernels, body(): pl.pallas_call(layer_kernel, out_shape=(jax.ShapeDtypeStruct((R, D), bf16...  190 us
    pallas_call x1, Pallas kernels, body(): pl.pallas_call(widen_kernel, out_shape=(jax.ShapeDtypeStruct((R, D), bf16...  9.22 us

profile of v2, /device:TPU:0, one launch (start us, length us, event | category | flops | bytes accessed | tf_op | source)
XLA Modules:
  0.0 200.0 jit_solution(2443631144404366648)
XLA Ops:
  0.6 190.1 %shard_map.220 = (bf16[512,768]{1,0:T(8,128)(2,1)}, bf16[512,768]{1,0:T(8,128)(2,1)}, bf16[2,2,768,768]{3,2,1,0:T(8,128)(2,1)}, bf16[4,2,96,768]{3,2,1,0:T(8,128)(2,1)}, f32[8,768]{1,0:T(8,128)}) custom-call(bf16[512,768]{1,0:T(8,128)(2,1)} %x_hbm.1, bf16[512,768]{1,0:T(8,128)(2,1)} %og_hbm.1, bf16[768,768]{1,0:T(8,128)(2,1)} %gate_hbm.1, ...), custom_call_target="tpu_custom_call" | custom-call | tf_op jit(solution)/shard_map/pallas_call | solution.py:987
  190.8 9.2 %shard_map.221 = (bf16[512,768]{1,0:T(8,128)(2,1)}, bf16[512,768]{1,0:T(8,128)(2,1)}, f32[768]{0:T(1024)}, f32[576,768]{1,0:T(8,128)}, f32[576,768]{1,0:T(8,128)...) custom-call(bf16[512,768]{1,0:T(8,128)(2,1)} %get-tuple-element.29.o, ...), custom_call_target="tpu_custom_call" | custom-call | tf_op jit(solution)/shard_map/pallas_call | solution.py:1009

commit v3 on v2

--- a/solution.py
+++ b/solution.py
@@ -19,42 +19,40 @@
 MESH = pl.DeviceIdType.MESH
 
 AFTER = {
-    "A0p1": (("zw", 0, 1), ("ag1", 0), ("zw", 0, 2),),
-    "A0p2": (("ag2", 0), ("zw", 0, 3), ("ag1", 1), ("ag3", 0), ("zs", 1),),
-    "A0p3": (("ag1", 2),),
-    "A0s": (("ag2", 1),),
-    "gate": (("ag2", 2),),
-    "A1p0": (("zw", 1, 1),),
-    "A1p1": (("zw", 1, 2), ("ag1", 3),),
-    "A1p3": (("ag3", 1),),
-    "A2q": (("zw", 1, 3), ("ag1", 4),),
-    "A2p0": (("ag3", 2),),
-    "A2s": (("ag2", 3),),
-    "A3p3": (("ag1", 5), ("ag2", 4),),
+    "A0p1": (("zw", 0, 1), ("ag1", 0), ("zw", 0, 2), ("zs", 1), ("ag2", 0), ("ag1", 1), ("zw", 1, 1), ("zw", 0, 3),),
+    "A0p2": (("zw", 1, 2), ("ag1", 3),),
+    "A0p3": (("ag3", 0), ("ag2", 1),),
+    "A1q": (("ag1", 2), ("ag3", 1), ("zw", 1, 3), ("ag1", 4),),
+    "A1p1": (("ag2", 2),),
+    "A2p1": (("ag1", 5),),
+    "A2s": (("ag2", 3), ("ag2", 4), ("ag3", 2), ("ag2", 5),),
     "F0a": (("ag3", 3),),
-    "F1a": (("rs0", 0), ("ag2", 5),),
-    "F1b": (("ag3", 4),),
-    "F1c": (("rs0", 1), ("rs1", 0),),
-    "F2a": (("rs1", 1), ("ag3", 5),),
-    "F3a": (("rs0", 2),),
-    "F3c": (("rs0", 3), ("rs1", 2),),
+    "F0c": (("rs0", 0),),
+    "F1a": (("ag3", 4),),
+    "F1c": (("rs1", 0), ("rs0", 1),),
+    "F2a": (("ag3", 5),),
+    "F2b": (("rs1", 1),),
+    "F2c": (("rs0", 2),),
+    "F3a": (("rs2", 0),),
+    "F3b": (("rs1", 2),),
+    "F3c": (("rs0", 3), ("rs2", 1),),
     "mid2": (("rs1", 3),),
-    "ggrad": (("rs2", 0), ("rs2", 2), ("g", 0), ("rs0", 4),),
-    "B0p3": (("rs1", 4),),
-    "B1o": (("rs2", 3),),
-    "B1p0": (("rs3", 0), ("rs0", 5),),
-    "B1p2": (("rs3", 2), ("rs1", 5),),
-    "B1p3": (("rs2", 1),),
-    "B2o": (("rs3", 3), ("rs0", 6),),
-    "B2p0": (("rs2", 4), ("zza", 0, 2),),
-    "B2p2": (("rs3", 1), ("rs1", 6),),
-    "B2g": (("zza", 0, 3), ("g", 1), ("rs0", 7), ("rs2", 5),),
-    "B2h": (("rs1", 7), ("rs3", 4),),
-    "B3p1": (("rs3", 5), ("g", 2), ("rs2", 6),),
-    "B3p3": (("fin0", 0),),
-    "B3g": (("rs0", 8), ("zza", 1, 3), ("rs2", 7), ("g", 3), ("rs3", 6), ("zza", 2, 3), ("rs1", 8), ("fin1", 0), ("zza", 1, 2),),
-    "B3h": (("g", 4),),
-    "tail": (("g", 5), ("zza", 2, 2), ("rs3", 7), ("rs2", 8), ("v", 0), ("fin2", 0), ("v", 1), ("fin0", 1), ("g", 6), ("rs3", 8), ("fin0", 2), ("v", 2), ("fin1", 1), ("fin1", 2), ("v", 3), ("v", 4), ("fin3", 0), ("fin2", 1), ("g", 7), ("fin2", 2), ("g", 8), ("fin3", 1), ("fin3", 2),),
+    "outmm": (("rs0", 4), ("rs2", 2),),
+    "B0o": (("g", 0),),
+    "B0p1": (("rs1", 4),),
+    "B0p2": (("rs3", 0), ("zfa", 0, 2), ("g", 1),),
+    "B0h": (("rs0", 5), ("rs2", 3),),
+    "B1p1": (("rs1", 5),),
+    "B1p3": (("zfa", 0, 3), ("rs3", 1),),
+    "B1g": (("rs0", 6), ("rs2", 4),),
+    "B1h": (("g", 2),),
+    "B2o": (("rs3", 3), ("rs2", 5), ("rs1", 6), ("rs3", 2),),
+    "B2g": (("rs0", 7), ("zza", 0, 3), ("g", 3), ("rs1", "z0"),),
+    "B2h": (("rs1", 7), ("rs3", 5), ("rs2", 6),),
+    "B3p0": (("rs2", "z0"), ("zza", 0, 2), ("rs3", 4),),
+    "B3g": (("rs0", 8), ("rs2", 7), ("rs1", 8), ("zza", 1, 2), ("rs3", 6),),
+    "B3h": (("rs3", "z0"), ("zza", 1, 3), ("zza", 2, 3), ("fin0", 0),),
+    "tail": (("g", 4), ("rs2", 8), ("zza", 2, 2), ("v", 0), ("rs3", 7), ("fin0", 1), ("fin1", 0), ("rs3", 8), ("g", 5), ("v", 1), ("fin0", 2), ("fin2", 0), ("fin1", 1), ("g", 6), ("v", 2), ("fin1", 2), ("v", 3), ("fin2", 1), ("fin3", 1), ("g", 7), ("v", 4), ("fin2", 2), ("g", 8), ("fin3", 0), ("fin3", 2),),
 }
 
 
@@ -80,10 +78,10 @@
     sq_ref, cq_ref, so_ref, co_ref, up_ref, dn_ref,
     out_hbm, tg_hbm, fin, gout, vec_ref,
     buf, crecv, p1a, p1b, p2a, p2b, cr_o, p1a_o, p1b_o, p2a_o, p2b_o,
-    z_f, z_o, z_q, e_f, e_o, e_q, gg, gcr, gxr, gyr, gzr, vs, vr, vz,
+    z_f, z_o, z_q, e_f, e_o, e_q, zr, ze, p1a_z, p1b_z, p2a_z, p2b_z, gg, gcr, gxr, gyr, gzr, vs, vr, vz,
     og_ref, bias_ref, h, qkv, o, lse, sc, aa, mid, h2, acc, gh, eb, wb,
     io, loc, az_s, az_r, a1_s, a1_r, a2_s, a2_r, ac_s, ac_r,
-    rc_s, rc_r, r1_s, r1_r, r2_s, r2_r, rz_s, rz_r, re_r,
+    rc_s, rc_r, r1_s, r1_r, r2_s, r2_r, rz_s, rz_r, re_r, zf_s, zf_r, zfe_r,
     f1_s, f1_r, f2_s, f2_r, fc_s, fc_r, fl,
     g_s, g_r, gz_s, gz_r, ga_s, ga_r, gl, v_s, v_r, vz_s, vz_r,
 ):
@@ -93,6 +91,7 @@
     gz = og_ref
     CH = buf.shape[3]
     XH, YH = CH // 2, D // 2
+    ZF = zr.shape[2]
     AR = XH // 2
     QR = sq_ref.shape[0]
     F = QR // 3
@@ -271,14 +270,23 @@
             add_rows(buf, (b, c, kq), r0, n, c0, w, src, idx)
 
         return dict(
-            reg=reg, add=add, nr=nr, ha=ha, sem=sem,
+            reg=reg, add=add, nr=nr, ha=ha, off=0, sem=sem,
             cr=(crecv, (slot,), pl.ds(0, nr)), a1=(p1a, (slot,), pl.ds(0, ha)),
             b1=[(p1b, (slot, xx), pl.ds(0, ha)) for xx in range(2)],
             a2=(p2a, (slot,), pl.ds(0, ha)), b2=(p2b, (slot,), pl.ds(0, ha)),
         )
 
     def k_ffn(k):
-        return single(2, CH, AR, k, k, k)
+        return single(2, CH, (XH - ZF) // 2, k, k, k)
+
+    def k_first():
+        kd = k_ffn(0)
+        every = slice(None)
+        kd.update(
+            off=XH - ZF, ha=ZF // 2, sem=9, a1=(p1a_z, (), every), b1=[(p1b_z, (xx,), every) for xx in range(2)],
+            a2=(p2a_z, (), every), b2=(p2b_z, (), every),
+        )
+        return kd
 
     def k_qkv(i):
         return single(1, QR, QR // 4, 3 - i, i, 5 + i)
@@ -293,7 +301,7 @@
 
         every = slice(None)
         return dict(
-            reg=reg, add=add, nr=F, ha=F // 4, sem=4,
+            reg=reg, add=add, nr=F, ha=F // 4, off=0, sem=4,
             cr=(cr_o, (), every), a1=(p1a_o, (), every), b1=[(p1b_o, (xx,), every) for xx in range(2)],
             a2=(p2a_o, (), every), b2=(p2b_o, (), every),
         )
@@ -307,19 +315,19 @@
         return remote(kd["reg"](1 - c, 0, kd["nr"], 0, D), land(kd["cr"]), rc_s.at[n], rc_r.at[n], dev_c)
 
     def rs_p1(kd):
-        n, half, ha, reg = kd["sem"], kd["nr"] // 2, kd["ha"], kd["reg"]
-        cps = [remote(reg(c, half * (1 - x), ha, 0, D), land(kd["a1"]), r1_s.at[n, 0], r1_r.at[n, 0], dev_x)]
+        n, half, ha, reg, off = kd["sem"], kd["nr"] // 2, kd["ha"], kd["reg"], kd["off"]
+        cps = [remote(reg(c, half * (1 - x) + off, ha, 0, D), land(kd["a1"]), r1_s.at[n, 0], r1_r.at[n, 0], dev_x)]
         for xx in range(2):
-            src = reg(c, half * xx + ha, ha, YH * (1 - y), YH)
+            src = reg(c, half * xx + off + ha, ha, YH * (1 - y), YH)
             cps.append(remote(src, land(kd["b1"][xx]), r1_s.at[n, 1 + xx], r1_r.at[n, 1 + xx], dev_y))
         return cps
 
     def rs_p2(kd):
-        n, half, ha, reg = kd["sem"], kd["nr"] // 2, kd["ha"], kd["reg"]
+        n, half, ha, reg, off = kd["sem"], kd["nr"] // 2, kd["ha"], kd["reg"], kd["off"]
         return [
-            remote(reg(c, half * x, ha, YH * (1 - y), YH), land(kd["a2"]), r2_s.at[n, 0], r2_r.at[n, 0], dev_y),
+            remote(reg(c, half * x + off, ha, YH * (1 - y), YH), land(kd["a2"]), r2_s.at[n, 0], r2_r.at[n, 0], dev_y),
             remote(
-                reg(c, half * (1 - x) + ha, ha, YH * y, YH), land(kd["b2"]), r2_s.at[n, 1], r2_r.at[n, 1], dev_x
+                reg(c, half * (1 - x) + off + ha, ha, YH * y, YH), land(kd["b2"]), r2_s.at[n, 1], r2_r.at[n, 1], dev_x
             ),
         ]
 
@@ -337,41 +345,45 @@
         cp.wait_send()
 
     def rs_2(kd):
-        half, ha = kd["nr"] // 2, kd["ha"]
+        half, ha, off = kd["nr"] // 2, kd["ha"], kd["off"]
         cps = rs_p1(kd)
         for q in cps:
             q.wait_recv()
-        kd["add"](half * x, ha, 0, D, kd["a1"][0], kd["a1"][1])
+        kd["add"](half * x + off, ha, 0, D, kd["a1"][0], kd["a1"][1])
         for xx in range(2):
-            kd["add"](half * xx + ha, ha, YH * y, YH, kd["b1"][xx][0], kd["b1"][xx][1])
+            kd["add"](half * xx + off + ha, ha, YH * y, YH, kd["b1"][xx][0], kd["b1"][xx][1])
         for q in rs_p2(kd):
             q.start()
         for q in cps:
             q.wait_send()
 
     def rs_3(kd, after=None):
-        half, ha = kd["nr"] // 2, kd["ha"]
+        half, ha, off = kd["nr"] // 2, kd["ha"], kd["off"]
         cps = rs_p2(kd)
         for q in cps:
             q.wait_recv()
-        kd["add"](half * x, ha, YH * y, YH, kd["a2"][0], kd["a2"][1])
-        kd["add"](half * x + ha, ha, YH * y, YH, kd["b2"][0], kd["b2"][1])
+        kd["add"](half * x + off, ha, YH * y, YH, kd["a2"][0], kd["a2"][1])
+        kd["add"](half * x + off + ha, ha, YH * y, YH, kd["b2"][0], kd["b2"][1])
         if after is not None:
             after()
         for q in cps:
             q.wait_send()
 
-    groups = ((2, 0, XH, z_f, e_f), (1, QR, F // 2, z_o, e_o), (1, 0, QR // 2, z_q, e_q))
+    groups = (
+        (2, 0, XH, XH - ZF, z_f, e_f),
+        (1, QR, F // 2, F // 2, z_o, e_o),
+        (1, 0, QR // 2, QR // 2, z_q, e_q),
+    )
 
     def z_part(gi, k):
-        b, r0, half = groups[gi][:3]
-        return buf.at[b, c, k, blk(r0 + half * x, half, 16), blk(YH * y, YH, 128)]
+        b, r0, half, n = groups[gi][:4]
+        return buf.at[b, c, k, blk(r0 + half * x, n, 16), blk(YH * y, YH, 128)]
 
     def z_out(gi, k):
-        return remote(z_part(gi, k), groups[gi][3].at[0 if k == 1 else 1], rz_s.at[gi, k], rz_r.at[gi, 0 if k == 1 else 1], (dp, zof(k)))
+        return remote(z_part(gi, k), groups[gi][4].at[0 if k == 1 else 1], rz_s.at[gi, k], rz_r.at[gi, 0 if k == 1 else 1], (dp, zof(k)))
 
     def z_hop(gi, k):
-        return remote(z_part(gi, k), groups[gi][4].at[k - 2], rz_s.at[gi, k], re_r.at[gi, k - 2], (dp, zof(1)))
+        return remote(z_part(gi, k), groups[gi][5].at[k - 2], rz_s.at[gi, k], re_r.at[gi, k - 2], (dp, zof(1)))
 
     def z_start(gi, k):
         if k == 1:
@@ -383,13 +395,50 @@
                 z_hop(gi, k).start()
 
     def z_join(gi, k):
-        b, r0, half, _to, mid_buf = groups[gi]
+        b, r0, half, n, _to, mid_buf = groups[gi]
 
         @pl.when(ismid == 1)
         def _():
             z_hop(gi, k).wait_recv()
-            add_rows(buf, (b, c, k), r0 + half * x, half, YH * y, YH, mid_buf, (k - 2,))
+            add_rows(buf, (b, c, k), r0 + half * x, n, YH * y, YH, mid_buf, (k - 2,))
             z_out(gi, k).start()
+
+    def zf_rows(k, xx):
+        return buf.at[2, c, k, pl.ds(XH * (xx + 1) - ZF, ZF), :]
+
+    def zf_out(k, xx):
+        to = 0 if k == 1 else 1
+        return remote(zf_rows(k, xx), zr.at[to, xx], zf_s.at[k, xx], zf_r.at[to, xx], (dp, zof(k)))
+
+    def zf_hop(k, xx):
+        return remote(zf_rows(k, xx), ze.at[k - 2, xx], zf_s.at[k, xx], zfe_r.at[k - 2, xx], (dp, zof(1)))
+
+    def zf_start(k):
+        if k == 1:
+            for xx in range(2):
+                zf_out(1, xx).start()
+        if k > 1:
+
+            @pl.when(ismid == 0)
+            def _():
+                for xx in range(2):
+                    zf_hop(k, xx).start()
+
+    def zf_join(_gi, k):
+        @pl.when(ismid == 1)
+        def _():
+            for xx in range(2):
+                zf_hop(k, xx).wait_recv()
+                add_rows(buf, (2, c, k), XH * (xx + 1) - ZF, ZF, 0, D, ze, (k - 2, xx))
+                zf_out(k, xx).start()
+
+    def zf_sum():
+        for xx in range(2):
+            for slot in range(2):
+                zf_out(1 + slot, xx).wait_recv()
+                add_rows(buf, (2, c, 0), XH * (xx + 1) - ZF, ZF, 0, D, zr, (slot, xx))
+        for q in rs_p1(k_first()):
+            q.start()
 
     def fin_part(gi, r, n, c0, w):
         r0 = groups[gi][1]
@@ -432,16 +481,19 @@
         return remote(ref, ref, fc_s.at[gi], fc_r.at[gi], dev_c)
 
     def fin_0(gi):
-        b, r0, half, part, _mid = groups[gi]
+        b, r0, half, n, part, _mid = groups[gi]
         for k in (1, 2):
             z_out(gi, k).wait_recv()
         for slot in range(2):
-            add_rows(buf, (b, c, 0), r0 + half * x, half, YH * y, YH, part, (slot,))
+            add_rows(buf, (b, c, 0), r0 + half * x, n, YH * y, YH, part, (slot,))
         for q in fin_p1(gi):
             q.start()
         fin_local(gi).start()
         for k in (1, 2, 3):
             z_out(gi, k).wait_send()
+            if gi == 0:
+                for xx in range(2):
+                    zf_out(k, xx).wait_send()
 
     def fin_1(gi):
         for q in fin_p1(gi):
@@ -572,10 +624,20 @@
                 v_z(slot, z, slot).wait_send()
 
     def kind(n):
+        if n == "z0":
+            return k_first()
         return k_ffn(n) if n < 4 else k_out() if n == 4 else k_qkv(n - 5)
 
+    def first(n):
+        if n == "z0":
+            zf_sum()
+        else:
+            rs_1(kind(n), lambda: zf_start(n) if n < 4 else None)
+
     def third(n):
-        if n < 4:
+        if n == "z0":
+            rs_3(kind(n))
+        elif n < 4:
             rs_3(kind(n), lambda: z_start(0, n))
         elif n == 4:
             rs_3(kind(n), lambda: [z_start(1, q) for q in range(1, 4)])
@@ -584,8 +646,8 @@
 
     events = {
         "zs": ag_zsend, "zw": ag_forward, "ag1": ag_1, "ag2": ag_2, "ag3": ag_3,
-        "rs0": lambda n: rs_0(kind(n)), "rs1": lambda n: rs_1(kind(n)), "rs2": lambda n: rs_2(kind(n)), "rs3": third,
-        "zza": z_join, "g": g_step, "v": v_step, "fin0": fin_0, "fin1": fin_1, "fin2": fin_2, "fin3": fin_3,
+        "rs0": lambda n: rs_0(kind(n)), "rs1": first, "rs2": lambda n: rs_2(kind(n)), "rs3": third,
+        "zza": z_join, "zfa": zf_join, "g": g_step, "v": v_step, "fin0": fin_0, "fin1": fin_1, "fin2": fin_2, "fin3": fin_3,
     }
 
     def after(name, k=None, p=None):
@@ -603,7 +665,7 @@
                         for ev in found:
                             events[ev[0]](*ev[1:])
 
-    TR = 64
+    TR = 128
     again = again_ref[...].astype(f32).reshape(1, D)
     fgain = fgain_ref[...].astype(f32).reshape(1, D)
     gbias = gbias_ref[...].astype(f32).reshape(1, D)
@@ -612,6 +674,8 @@
     for cp in local[:4]:
         cp.wait()
     ag_zsend(0)
+
+    after("start")
 
     key_id = lax.broadcasted_iota(jnp.int32, (SLOTS, SLOTS), 0)
     query_id = lax.broadcasted_iota(jnp.int32, (SLOTS, SLOTS), 1)
@@ -654,23 +718,28 @@
         @pl.loop(0, pages)
         def _(p):
             cols = blk(p * SLOTS, SLOTS, 128)
-            for at in range(2):
-                for hh in range(heads):
-                    qt = qkv[at, k, HEAD * hh : HEAD * (hh + 1), cols]
-                    kt = qkv[at, k, F + HEAD * hh : F + HEAD * (hh + 1), cols]
-                    vt = qkv[at, k, 2 * F + HEAD * hh : 2 * F + HEAD * (hh + 1), cols]
-                    st = mm(kt, qt, "tn") * HEAD ** (-0.5) + bias_ref[at, p].astype(f32)
-                    top = jnp.max(st, axis=0, keepdims=True)
-                    ex = jnp.exp(st - top)
-                    tot = jnp.sum(ex, axis=0, keepdims=True)
-                    pt = (ex * (1.0 / tot)).astype(bf16)
-                    lse[at, k, hh : hh + 1, cols] = top + jnp.log(tot)
-                    o[at, k, HEAD * hh : HEAD * (hh + 1), cols] = mm(vt, pt, "nn").astype(bf16)
+            units = [(at, hh) for at in range(2) for hh in range(heads)]
+            scores = []
+            for at, hh in units:
+                qt = qkv[at, k, HEAD * hh : HEAD * (hh + 1), cols]
+                kt = qkv[at, k, F + HEAD * hh : F + HEAD * (hh + 1), cols]
+                scores.append(mm(kt, qt, "tn"))
+            probs = []
+            for (at, hh), st in zip(units, scores):
+                st = st * HEAD ** (-0.5) + bias_ref[at, p].astype(f32)
+                top = jnp.max(st, axis=0, keepdims=True)
+                ex = jnp.exp(st - top)
+                tot = jnp.sum(ex, axis=0, keepdims=True)
+                probs.append((ex * (1.0 / tot)).astype(bf16))
+                lse[at, k, hh : hh + 1, cols] = top + jnp.log(tot)
+            for (at, hh), pt in zip(units, probs):
+                vt = qkv[at, k, 2 * F + HEAD * hh : 2 * F + HEAD * (hh + 1), cols]
+                o[at, k, HEAD * hh : HEAD * (hh + 1), cols] = mm(vt, pt, "nn").astype(bf16)
             after("Ap", k, p)
 
-        @pl.loop(0, pages)
+        @pl.loop(0, 2)
         def _(p):
-            cols = blk(p * SLOTS, SLOTS, 128)
+            cols = blk(p * 256, 256, 128)
             for at, dst in ((0, sc), (1, mid)):
                 dst[cols, :] += mm(o[at, k, :, cols], buf[0, at, zz, QR:CH, :], "tn")
 
@@ -678,9 +747,9 @@
 
         @pl.when(k == 0)
         def _():
-            @pl.loop(0, R // 128)
+            @pl.loop(0, R // 256)
             def _(i):
-                rows = blk(i * 128, 128, 16)
+                rows = blk(i * 256, 256, 16)
                 aa[rows, :] = jax.nn.sigmoid(mm(h[rows, :], gate_ref[...], "nn") + gbias)
 
             after("gate")
@@ -711,17 +780,18 @@
 
         MT = 256
 
-        @pl.loop(0, R // MT)
+        @pl.loop(0, 2 * (R // MT))
         def _(i):
-            rows = blk(i * MT, MT, 16)
-            w = mm(h2[rows, :], buf[1, 0, zz], "nn")
-            ge = mm(og_ref[rows, :], buf[1, 1, zz], "nt")
+            rows = blk((i // 2) * MT, MT, 16)
+            cols = blk((i % 2) * XH, XH, 128)
+            w = mm(h2[rows, :], buf[1, 0, zz, :, cols], "nn")
+            ge = mm(og_ref[rows, :], buf[1, 1, zz, blk((i % 2) * XH, XH, 16), :], "nt")
             w2 = w * w
             th = jnp.tanh(GC * w * (1.0 + GK * w2))
             half = 0.5 * (1.0 + th)
-            eb[rows, :] = (w * half).astype(bf16)
+            eb[rows, cols] = (w * half).astype(bf16)
             dg = half + 0.5 * w * (1.0 - th * th) * (GC * (1.0 + 3.0 * GK * w2))
-            wb[rows, :] = (dg * ge).astype(bf16)
+            wb[rows, cols] = (dg * ge).astype(bf16)
 
         after("Fa", k)
 
@@ -733,17 +803,17 @@
 
         after("Fb", k)
 
-        @pl.loop(0, CH // 256)
+        @pl.loop(0, CH // 384)
         def _(i):
-            cols = blk(i * 256, 256, 128)
-            buf[2, 1, k, blk(i * 256, 256, 16), :] = mm(eb[:, cols], og_ref[...], "tn").astype(bf16)
-            buf[2, 0, k, blk(i * 256, 256, 16), :] = mm(h2[:, cols], wb[...], "tn").astype(bf16)
+            cols = blk(i * 384, 384, 128)
+            buf[2, 1, k, blk(i * 384, 384, 16), :] = mm(eb[:, cols], og_ref[...], "tn").astype(bf16)
+            buf[2, 0, k, blk(i * 384, 384, 16), :] = mm(h2[:, cols], wb[...], "tn").astype(bf16)
 
         after("Fc", k)
 
     ag_zsend_wait(1)
 
-    TS = 32
+    TS = 128
     zero_row = jnp.zeros((1, D), f32)
 
     def mid_back(i, sums):
@@ -805,26 +875,25 @@
         @pl.loop(0, pages)
         def _(p):
             cols = blk(p * SLOTS, SLOTS, 128)
-            for at in range(2):
-                for hh in range(heads):
+            units = [(at, hh) for at in range(2) for hh in range(heads)]
+            for grp in (units,):
+                rd = []
+                for at, hh in grp:
                     qs = slice(HEAD * hh, HEAD * (hh + 1))
                     ks = slice(F + HEAD * hh, F + HEAD * (hh + 1))
                     vsl = slice(2 * F + HEAD * hh, 2 * F + HEAD * (hh + 1))
-                    qt = qkv[at, k, qs, cols]
-                    kt = qkv[at, k, ks, cols]
-                    vt = qkv[at, k, vsl, cols]
-                    go = o[at, k, qs, cols]
-                    st = mm(kt, qt, "tn") * HEAD ** (-0.5) + bias_ref[at, p].astype(f32)
-                    pt = jnp.exp(st - lse[at, k, hh : hh + 1, cols])
-                    gvt = mm(go, pt.astype(bf16), "nt")
-                    gpt = mm(vt, go, "tn")
+                    qt, kt, vt, go = qkv[at, k, qs, cols], qkv[at, k, ks, cols], qkv[at, k, vsl, cols], o[at, k, qs, cols]
+                    rd.append((at, hh, qs, ks, vsl, qt, kt, vt, go, mm(kt, qt, "tn"), mm(vt, go, "tn")))
+                ps = []
+                for at, hh, qs, ks, vsl, qt, kt, vt, go, st, gpt in rd:
+                    pt = jnp.exp(st * HEAD ** (-0.5) + bias_ref[at, p].astype(f32) - lse[at, k, hh : hh + 1, cols])
                     pg = pt * gpt
                     gst = (pg - pt * jnp.sum(pg, axis=0, keepdims=True)).astype(bf16)
-                    gqt = mm(kt, gst, "nn") * HEAD ** (-0.5)
-                    gkt = mm(qt, gst, "nt") * HEAD ** (-0.5)
-                    qkv[at, k, qs, cols] = gqt.astype(bf16)
-                    qkv[at, k, ks, cols] = gkt.astype(bf16)
-                    qkv[at, k, vsl, cols] = gvt.astype(bf16)
+                    ps.append((pt.astype(bf16), gst))
+                for (at, hh, qs, ks, vsl, qt, kt, vt, go, st, gpt), (pb, gst) in zip(rd, ps):
+                    qkv[at, k, vsl, cols] = mm(go, pb, "nt").astype(bf16)
+                    qkv[at, k, qs, cols] = (mm(kt, gst, "nn") * HEAD ** (-0.5)).astype(bf16)
+                    qkv[at, k, ks, cols] = (mm(qt, gst, "nt") * HEAD ** (-0.5)).astype(bf16)
             after("Bp", i, p)
 
         for at in range(2):
@@ -833,9 +902,9 @@
                 buf[1, at, k, part, :] = mm(qkv[at, k, part, :], h[...], "nn").astype(bf16)
         after("Bg", i)
 
-        @pl.loop(0, pages)
+        @pl.loop(0, 2)
         def _(p):
-            cols = blk(p * SLOTS, SLOTS, 128)
+            cols = blk(p * 256, 256, 128)
             t = mm(qkv[0, k, :, cols], buf[0, 0, zz, 0:QR, :], "tn") + mm(qkv[1, k, :, cols], buf[0, 1, zz, 0:QR, :], "tn")
 
             @pl.when(i == 0)
@@ -850,9 +919,9 @@
 
     gate_load.wait()
 
-    @pl.loop(0, R // 128)
+    @pl.loop(0, R // 256)
     def _(i):
-        rows = blk(i * 128, 128, 16)
+        rows = blk(i * 256, 256, 16)
         gh[rows, :] += mm(gz[rows, :], gate_again[...], "nt")
 
     def first_back(i, gain_sum):
@@ -886,9 +955,13 @@
     for i, (src, dst) in enumerate(((out_in, out_o), (tg_in, tg_o))):
         load = pltpu.make_async_copy(src, whole.at[i], sem_pass.at[i])
         passes.append((load, pltpu.make_async_copy(whole.at[i], dst, sem_pass.at[2 + i])))
-    parts = [(fin.at[0, 0], up_o), (fin.at[0, 1], dn_o), (gout, gw_o)]
+    parts = []
+    for src, dst in ((fin.at[0, 0], up_o), (fin.at[0, 1], dn_o), (gout, gw_o)):
+        n = src.shape[0] // 3
+        parts += [(src.at[pl.ds(n * q, n)], dst.at[pl.ds(n * q, n)]) for q in range(3)]
     for cc, (a, b) in enumerate(((sq_o, so_o), (cq_o, co_o))):
-        parts += [(fin.at[1, cc, pl.ds(0, QR)], a), (fin.at[1, cc, pl.ds(QR, F)], b)]
+        parts += [(fin.at[1, cc, pl.ds(QR, F)], b)]
+        parts += [(fin.at[1, cc, pl.ds(F * q, F)], a.at[pl.ds(F * q, F)]) for q in range(3)]
     r0 = 0
     jobs = []
     for i, (src, dst) in enumerate(parts):
@@ -934,25 +1007,31 @@
     vm = pl.BlockSpec(memory_space=pltpu.VMEM)
     hb = pl.BlockSpec(memory_space=pl.ANY)
     dma = pltpu.SemaphoreType.DMA
-    XH, YH, AR, GX, OR = CH // 2, D // 2, CH // 4, D // 16, F // 4
+    XH, YH, GX, OR, ZF = CH // 2, D // 2, D // 16, F // 4, CH // 6
     scratch = [
         pltpu.VMEM((3, 2, 4, CH, D), bf16),
         pltpu.VMEM((4, CH, D), bf16),
-        pltpu.VMEM((4, AR, D), bf16),
-        pltpu.VMEM((4, 2, AR, YH), bf16),
-        pltpu.VMEM((4, AR, YH), bf16),
-        pltpu.VMEM((4, AR, YH), bf16),
+        pltpu.VMEM((4, QR // 4, D), bf16),
+        pltpu.VMEM((4, 2, QR // 4, YH), bf16),
+        pltpu.VMEM((4, QR // 4, YH), bf16),
+        pltpu.VMEM((4, QR // 4, YH), bf16),
         pltpu.VMEM((4, F, D), bf16),
         pltpu.VMEM((4, OR, D), bf16),
         pltpu.VMEM((2, 4, OR, YH), bf16),
         pltpu.VMEM((4, OR, YH), bf16),
         pltpu.VMEM((4, OR, YH), bf16),
-        pltpu.VMEM((2, XH, YH), bf16),
+        pltpu.VMEM((2, XH - ZF, YH), bf16),
         pltpu.VMEM((2, F // 2, YH), bf16),
         pltpu.VMEM((2, QR // 2, YH), bf16),
-        pltpu.VMEM((2, XH, YH), bf16),
+        pltpu.VMEM((2, XH - ZF, YH), bf16),
         pltpu.VMEM((2, F // 2, YH), bf16),
         pltpu.VMEM((2, QR // 2, YH), bf16),
+        pltpu.VMEM((2, 2, ZF, D), bf16),
+        pltpu.VMEM((2, 2, ZF, D), bf16),
+        pltpu.VMEM((ZF // 2, D), bf16),
+        pltpu.VMEM((2, ZF // 2, YH), bf16),
+        pltpu.VMEM((ZF // 2, YH), bf16),
+        pltpu.VMEM((ZF // 2, YH), bf16),
         pltpu.VMEM((4, 2, 2 * GX, D), bf16),
         pltpu.VMEM((4, 2 * GX, D), bf16),
         pltpu.VMEM((4, GX, D), bf16),
@@ -978,8 +1057,8 @@
         dma((7,)),
         dma((6,)), dma((2, 5)), dma((2, 4)), dma((2, 4, 2)), dma((2, 4, 2)), dma((2, 4, 3)), dma((2, 4, 3)),
         dma((2, 4)), dma((2, 4)),
-        dma((9,)), dma((9,)), dma((9, 3)), dma((9, 3)), dma((9, 2)), dma((9, 2)), dma((3, 4)), dma((3, 2)),
-        dma((3, 2)),
+        dma((9,)), dma((9,)), dma((10, 3)), dma((10, 3)), dma((10, 2)), dma((10, 2)), dma((3, 4)), dma((3, 2)),
+        dma((3, 2)), dma((4, 2)), dma((2, 2)), dma((2, 2)),
         dma((3, 2)), dma((3, 2)), dma((3, 3)), dma((3, 3)), dma((3,)), dma((3,)), dma((3,)),
         dma((6,)), dma((6,)), dma((4,)), dma((4,)), dma((4,)), dma((4,)), dma((1,)),
         dma((3,)), dma((3,)), dma((4,)), dma((4,)),
@@ -1017,7 +1096,7 @@
         out_specs=(hb, hb, vm, hb, hb, hb, hb, hb, vm, vm, hb, hb),
         scratch_shapes=[
             pltpu.VMEM((total, D), bf16), pltpu.VMEM((total, D), f32), pltpu.VMEM((2, R, D), bf16),
-            dma((7,)), dma((7,)), dma((4,)),
+            dma((17,)), dma((17,)), dma((4,)),
         ],
         compiler_params=pltpu.CompilerParams(vmem_limit_bytes=60 * 2**20),
     )(out, tg, fin, gout.reshape(D, D), vec)

time: 200 us -> 191 us (0.955)
  Pallas kernels: 199 us -> 190 us
    pallas_call x1, Pallas kernels: 190 us -> 181 us  [body(): pl.pallas_call(layer_kernel, out_shape=(jax.ShapeDtypeStruct((R, D), bf16...]
where the time goes in v3:
time: 191 us
  Pallas kernels  190 us (99%)
    pallas_call x1, Pallas kernels, body(): pl.pallas_call(layer_kernel, out_shape=(jax.ShapeDtypeStruct((R, D), bf16...  181 us
    pallas_call x1, Pallas kernels, body(): pl.pallas_call(widen_kernel, out_shape=(jax.ShapeDtypeStruct((R, D), bf16...  9.36 us

profile of v3, /device:TPU:0, one launch (start us, length us, event | category | flops | bytes accessed | tf_op | source)
XLA Modules:
  0.0 191.0 jit_solution(3306471332593408856)
XLA Ops:
  0.6 180.8 %shard_map.220 = (bf16[512,768]{1,0:T(8,128)(2,1)}, bf16[512,768]{1,0:T(8,128)(2,1)}, bf16[2,2,768,768]{3,2,1,0:T(8,128)(2,1)}, bf16[4,2,96,768]{3,2,1,0:T(8,128)(2,1)}, f32[8,768]{1,0:T(8,128)}) custom-call(bf16[512,768]{1,0:T(8,128)(2,1)} %x_hbm.1, bf16[512,768]{1,0:T(8,128)(2,1)} %og_hbm.1, bf16[768,768]{1,0:T(8,128)(2,1)} %gate_hbm.1, ...), custom_call_target="tpu_custom_call" | custom-call | tf_op jit(solution)/shard_map/pallas_call | solution.py:1066
  181.4 9.4 %shard_map.221 = (bf16[512,768]{1,0:T(8,128)(2,1)}, bf16[512,768]{1,0:T(8,128)(2,1)}, f32[768]{0:T(1024)}, f32[576,768]{1,0:T(8,128)}, f32[576,768]{1,0:T(8,128)...) custom-call(bf16[512,768]{1,0:T(8,128)(2,1)} %get-tuple-element.29.o, ...), custom_call_target="tpu_custom_call" | custom-call | tf_op jit(solution)/shard_map/pallas_call | solution.py:1088

commit v4 on v3

--- a/solution.py
+++ b/solution.py
@@ -19,40 +19,49 @@
 MESH = pl.DeviceIdType.MESH
 
 AFTER = {
-    "A0p1": (("zw", 0, 1), ("ag1", 0), ("zw", 0, 2), ("zs", 1), ("ag2", 0), ("ag1", 1), ("zw", 1, 1), ("zw", 0, 3),),
-    "A0p2": (("zw", 1, 2), ("ag1", 3),),
-    "A0p3": (("ag3", 0), ("ag2", 1),),
-    "A1q": (("ag1", 2), ("ag3", 1), ("zw", 1, 3), ("ag1", 4),),
-    "A1p1": (("ag2", 2),),
-    "A2p1": (("ag1", 5),),
-    "A2s": (("ag2", 3), ("ag2", 4), ("ag3", 2), ("ag2", 5),),
+    "norm": (("agp", 1), ("agp", 0), ("agp", 2), ("agp", 3), ("zw", 0, 1), ("zw", 0, 2), ("ag2", 0),),
+    "A0p0": (("ag1", 1), ("zw", 0, 3), ("zs", 1),),
+    "A0p2": (("ag3", 0),),
+    "A0p3": (("ag2", 1),),
+    "A0s": (("zw", 1, 1),),
+    "gate": (("zw", 1, 2), ("ag1", 2),),
+    "A1p0": (("ag1", 3),),
+    "A1p1": (("zw", 1, 3), ("ag2", 2),),
+    "A1p3": (("ag3", 1),),
+    "A2q": (("ag1", 4),),
+    "A2p0": (("ag2", 3),),
+    "A2p1": (("ag3", 2), ("ag1", 5),),
+    "A2s": (("ag2", 4),),
     "F0a": (("ag3", 3),),
-    "F0c": (("rs0", 0),),
-    "F1a": (("ag3", 4),),
-    "F1c": (("rs1", 0), ("rs0", 1),),
-    "F2a": (("ag3", 5),),
-    "F2b": (("rs1", 1),),
+    "F0b": (("ag2", 5),),
+    "F1a": (("rs0", 0),),
+    "F1b": (("ag3", 4),),
+    "F1c": (("rs0", 1), ("rs1", 0),),
+    "F2a": (("rs1", 1), ("ag3", 5),),
     "F2c": (("rs0", 2),),
     "F3a": (("rs2", 0),),
     "F3b": (("rs1", 2),),
     "F3c": (("rs0", 3), ("rs2", 1),),
     "mid2": (("rs1", 3),),
-    "outmm": (("rs0", 4), ("rs2", 2),),
-    "B0o": (("g", 0),),
-    "B0p1": (("rs1", 4),),
-    "B0p2": (("rs3", 0), ("zfa", 0, 2), ("g", 1),),
-    "B0h": (("rs0", 5), ("rs2", 3),),
-    "B1p1": (("rs1", 5),),
-    "B1p3": (("zfa", 0, 3), ("rs3", 1),),
-    "B1g": (("rs0", 6), ("rs2", 4),),
-    "B1h": (("g", 2),),
-    "B2o": (("rs3", 3), ("rs2", 5), ("rs1", 6), ("rs3", 2),),
-    "B2g": (("rs0", 7), ("zza", 0, 3), ("g", 3), ("rs1", "z0"),),
-    "B2h": (("rs1", 7), ("rs3", 5), ("rs2", 6),),
-    "B3p0": (("rs2", "z0"), ("zza", 0, 2), ("rs3", 4),),
-    "B3g": (("rs0", 8), ("rs2", 7), ("rs1", 8), ("zza", 1, 2), ("rs3", 6),),
-    "B3h": (("rs3", "z0"), ("zza", 1, 3), ("zza", 2, 3), ("fin0", 0),),
-    "tail": (("g", 4), ("rs2", 8), ("zza", 2, 2), ("v", 0), ("rs3", 7), ("fin0", 1), ("fin1", 0), ("rs3", 8), ("g", 5), ("v", 1), ("fin0", 2), ("fin2", 0), ("fin1", 1), ("g", 6), ("v", 2), ("fin1", 2), ("v", 3), ("fin2", 1), ("fin3", 1), ("g", 7), ("v", 4), ("fin2", 2), ("g", 8), ("fin3", 0), ("fin3", 2),),
+    "outmm": (("rs0", 4),),
+    "B0o": (("rs3", 1), ("rs2", 2),),
+    "B0p0": (("rs3", 0),),
+    "B0p1": (("rs1", 4), ("zfa", 0, 2),),
+    "B0g": (("rs0", 5),),
+    "B1o": (("rs2", 3), ("g", 0), ("rs1", 5),),
+    "B1p2": (("zfa", 0, 3), ("g", 1),),
+    "B1g": (("rs0", 6), ("rs2", 4), ("rs3", 2),),
+    "B2o": (("rs2", 5), ("rs1", 6),),
+    "B2p0": (("g", 2),),
+    "B2p1": (("rs3", 3),),
+    "B2g": (("rs0", 7), ("rs3", 5), ("rs1", "z0"),),
+    "B2h": (("rs1", 7),),
+    "B3o": (("rs2", 6), ("zza", 0, 3),),
+    "B3p1": (("rs3", 4), ("rs2", "z0"),),
+    "B3p2": (("zza", 0, 2),),
+    "B3g": (("rs0", 8), ("g", 3), ("rs2", 7), ("zza", 2, 3), ("rs3", 6), ("rs1", 8), ("rs3", "z0"), ("zza", 1, 2),),
+    "B3h": (("fin0", 0), ("g", 4),),
+    "tail": (("v", 0), ("rs2", 8), ("zza", 2, 2), ("rs3", 7), ("g", 5), ("v", 1), ("fin1", 0), ("rs3", 8), ("zza", 1, 3), ("fin0", 2), ("g", 6), ("v", 2), ("fin0", 1), ("fin1", 2), ("g", 7), ("fin1", 1), ("v", 3), ("fin2", 0), ("fin2", 2), ("fin2", 1), ("fin3", 0), ("v", 4), ("fin3", 2), ("g", 8), ("fin3", 1),),
 }
 
 
@@ -80,7 +89,7 @@
     buf, crecv, p1a, p1b, p2a, p2b, cr_o, p1a_o, p1b_o, p2a_o, p2b_o,
     z_f, z_o, z_q, e_f, e_o, e_q, zr, ze, p1a_z, p1b_z, p2a_z, p2b_z, gg, gcr, gxr, gyr, gzr, vs, vr, vz,
     og_ref, bias_ref, h, qkv, o, lse, sc, aa, mid, h2, acc, gh, eb, wb,
-    io, loc, az_s, az_r, a1_s, a1_r, a2_s, a2_r, ac_s, ac_r,
+    io, loc, ap_s, ap_r, a0_s, a0_r, az_s, az_r, a1_s, a1_r, a2_s, a2_r, ac_s, ac_r,
     rc_s, rc_r, r1_s, r1_r, r2_s, r2_r, rz_s, rz_r, re_r, zf_s, zf_r, zfe_r,
     f1_s, f1_r, f2_s, f2_r, fc_s, fc_r, fl,
     g_s, g_r, gz_s, gz_r, ga_s, ga_r, gl, v_s, v_r, vz_s, vz_r,
@@ -158,15 +167,49 @@
         ref = wquarter(g, zz)
         return remote(ref, ref, az_s.at[g, sidx], az_r.at[g, rslot], (dp, zof(slot_to)))
 
+    PIECES = 4
+
+    def piece(zz, q):
+        n = AR // PIECES
+        out = []
+        for i in range(2):
+            ref = wpart(0, c, zz, XH * x + AR * i + n * q, n, YH * y, YH)
+            out.append(remote(ref, ref, ap_s.at[q, i], ap_r.at[q, i], (dp, zof(1))))
+        return out
+
+    def piece_p1(zz, xx, yy, q):
+        n = AR // PIECES
+        ra = wpart(0, c, zz, XH * xx + n * q, n, YH * y, YH)
+        rb = wpart(0, c, zz, XH * x + AR + n * q, n, YH * yy, YH)
+        return (
+            remote(ra, ra, a0_s.at[q, 0], a0_r.at[q, 0], dev_x), remote(rb, rb, a0_s.at[q, 1], a0_r.at[q, 1], dev_y)
+        )
+
+    def ag_piece(q):
+        for cp in piece(zof(1), q):
+            cp.wait_recv()
+        for cp in piece_p1(zof(1), x, y, q):
+            cp.start()
+
     def ag_zsend(g):
-        z_copy(g, z, 1, 0, 1).start()
+        if g == 0:
+            for q in range(PIECES):
+                for cp in piece(z, q):
+                    cp.start()
+        else:
+            z_copy(g, z, 1, 0, 1).start()
 
         @pl.when(ismid == 1)
         def _():
             z_copy(g, z, 2, 1, 2).start()
 
     def ag_zsend_wait(g):
-        z_copy(g, z, 1, 0, 1).wait_send()
+        if g == 0:
+            for q in range(PIECES):
+                for cp in piece(z, q):
+                    cp.wait_send()
+        else:
+            z_copy(g, z, 1, 0, 1).wait_send()
 
         @pl.when(ismid == 1)
         def _():
@@ -211,7 +254,8 @@
     def ag_forward(g, j):
         @pl.when(ismid == 1)
         def _():
-            z_copy(g, zof(j), 1, 0, j).wait_recv()
+            if g == 1 or j > 1:
+                z_copy(g, zof(j), 1, 0, j).wait_recv()
             if j == 1:
                 z_copy(g, zof(1), 2, 2, 3).start()
             else:
@@ -229,7 +273,11 @@
 
     def ag_2(t):
         g, j = t // 3, t % 3 + 1
-        outs, arrivals = ag_p1(g, j)
+        if t == 0:
+            outs = [cp for q in range(PIECES) for cp in piece_p1(zof(1), x, y, q)]
+            arrivals = [cp for q in range(PIECES) for cp in piece_p1(zof(1), 1 - x, 1 - y, q)]
+        else:
+            outs, arrivals = ag_p1(g, j)
         for cp in arrivals:
             cp.wait_recv()
         for cp in ag_p2(g, j)[0]:
@@ -645,7 +693,7 @@
             rs_3(kind(n), lambda: z_start(2, 8 - n))
 
     events = {
-        "zs": ag_zsend, "zw": ag_forward, "ag1": ag_1, "ag2": ag_2, "ag3": ag_3,
+        "zs": ag_zsend, "zw": ag_forward, "agp": ag_piece, "ag1": ag_1, "ag2": ag_2, "ag3": ag_3,
         "rs0": lambda n: rs_0(kind(n)), "rs1": first, "rs2": lambda n: rs_2(kind(n)), "rs3": third,
         "zza": z_join, "zfa": zf_join, "g": g_step, "v": v_step, "fin0": fin_0, "fin1": fin_1, "fin2": fin_2, "fin3": fin_3,
     }
@@ -955,41 +1003,42 @@
     for i, (src, dst) in enumerate(((out_in, out_o), (tg_in, tg_o))):
         load = pltpu.make_async_copy(src, whole.at[i], sem_pass.at[i])
         passes.append((load, pltpu.make_async_copy(whole.at[i], dst, sem_pass.at[2 + i])))
-    parts = []
-    for src, dst in ((fin.at[0, 0], up_o), (fin.at[0, 1], dn_o), (gout, gw_o)):
-        n = src.shape[0] // 3
-        parts += [(src.at[pl.ds(n * q, n)], dst.at[pl.ds(n * q, n)]) for q in range(3)]
-    for cc, (a, b) in enumerate(((sq_o, so_o), (cq_o, co_o))):
-        parts += [(fin.at[1, cc, pl.ds(QR, F)], b)]
-        parts += [(fin.at[1, cc, pl.ds(F * q, F)], a.at[pl.ds(F * q, F)]) for q in range(3)]
-    r0 = 0
+    CH = 4 * F
     jobs = []
-    for i, (src, dst) in enumerate(parts):
-        n = src.shape[0]
-        load = pltpu.make_async_copy(src, narrow.at[pl.ds(r0, n)], sem_in.at[i])
-        save = pltpu.make_async_copy(wide.at[pl.ds(r0, n)], dst, sem_out.at[i])
+    for i, (src, dsts) in enumerate(
+        (
+            (gout, ((0, gw_o),)), (fin.at[0, 0], ((0, up_o),)), (fin.at[0, 1], ((0, dn_o),)),
+            (fin.at[1, 0], ((0, sq_o), (QR, so_o))), (fin.at[1, 1], ((0, cq_o), (QR, co_o))),
+        )
+    ):
+        load = pltpu.make_async_copy(src, narrow.at[pl.ds(CH * i, CH)], sem_in.at[i])
+        saves = [
+            pltpu.make_async_copy(wide.at[pl.ds(CH * i + r0, dst.shape[0])], dst, sem_out.at[i, q])
+            for q, (r0, dst) in enumerate(dsts)
+        ]
         load.start()
-        jobs.append((r0, n, load, save))
-        r0 += n
+        jobs.append((load, saves))
     for load, _ in passes:
         load.start()
     ag_o[...] = vec_in[0, :]
     gb_o[...] = vec_in[1, :]
     fg_o[...] = vec_in[2, :]
+    for i, (load, saves) in enumerate(jobs):
+        load.wait()
+
+        @pl.loop(0, CH // 64)
+        def _(q):
+            rows = blk(CH * i + 64 * q, 64, 16)
+            wide[rows, :] = narrow[rows, :].astype(f32)
+
+        for cp in saves:
+            cp.start()
     for load, save in passes:
         load.wait()
         save.start()
-    for r0, n, load, save in jobs:
-        load.wait()
-
-        @pl.loop(0, n // 64)
-        def _(i):
-            rows = blk(r0 + 64 * i, 64, 16)
-            wide[rows, :] = narrow[rows, :].astype(f32)
-
-        save.start()
-    for _, _, _, save in jobs:
-        save.wait()
+    for _, saves in jobs:
+        for cp in saves:
+            cp.wait()
     for _, save in passes:
         save.wait()
 
@@ -1055,7 +1104,7 @@
         pltpu.VMEM((R, D), bf16),
         pltpu.VMEM((R, D), bf16),
         dma((7,)),
-        dma((6,)), dma((2, 5)), dma((2, 4)), dma((2, 4, 2)), dma((2, 4, 2)), dma((2, 4, 3)), dma((2, 4, 3)),
+        dma((6,)), dma((4, 2)), dma((4, 2)), dma((4, 2)), dma((4, 2)), dma((2, 5)), dma((2, 4)), dma((2, 4, 2)), dma((2, 4, 2)), dma((2, 4, 3)), dma((2, 4, 3)),
         dma((2, 4)), dma((2, 4)),
         dma((9,)), dma((9,)), dma((10, 3)), dma((10, 3)), dma((10, 2)), dma((10, 2)), dma((3, 4)), dma((3, 2)),
         dma((3, 2)), dma((4, 2)), dma((2, 2)), dma((2, 2)),
@@ -1096,7 +1145,7 @@
         out_specs=(hb, hb, vm, hb, hb, hb, hb, hb, vm, vm, hb, hb),
         scratch_shapes=[
             pltpu.VMEM((total, D), bf16), pltpu.VMEM((total, D), f32), pltpu.VMEM((2, R, D), bf16),
-            dma((17,)), dma((17,)), dma((4,)),
+            dma((5,)), dma((5, 2)), dma((4,)),
         ],
         compiler_params=pltpu.CompilerParams(vmem_limit_bytes=60 * 2**20),
     )(out, tg, fin, gout.reshape(D, D), vec)

time: 191 us -> 187 us (0.979)
  Pallas kernels: 190 us -> 186 us
    pallas_call x1, Pallas kernels: 181 us -> 178 us  [body(): pl.pallas_call(layer_kernel, out_shape=(jax.ShapeDtypeStruct((R, D), bf16...]
where the time goes in v4:
time: 187 us
  Pallas kernels  186 us (99%)
    pallas_call x1, Pallas kernels, body(): pl.pallas_call(layer_kernel, out_shape=(jax.ShapeDtypeStruct((R, D), bf16...  178 us
    pallas_call x1, Pallas kernels, body(): pl.pallas_call(widen_kernel, out_shape=(jax.ShapeDtypeStruct((R, D), bf16...  8.02 us

profile of v4, /device:TPU:0, one launch (start us, length us, event | category | flops | bytes accessed | tf_op | source)
XLA Modules:
  0.0 186.6 jit_solution(2787919363510942045)
XLA Ops:
  0.6 177.9 %shard_map.220 = (bf16[512,768]{1,0:T(8,128)(2,1)}, bf16[512,768]{1,0:T(8,128)(2,1)}, bf16[2,2,768,768]{3,2,1,0:T(8,128)(2,1)}, bf16[4,2,96,768]{3,2,1,0:T(8,128)(2,1)}, f32[8,768]{1,0:T(8,128)}) custom-call(bf16[512,768]{1,0:T(8,128)(2,1)} %x_hbm.1, bf16[512,768]{1,0:T(8,128)(2,1)} %og_hbm.1, bf16[768,768]{1,0:T(8,128)(2,1)} %gate_hbm.1, ...), custom_call_target="tpu_custom_call" | custom-call | tf_op jit(solution)/shard_map/pallas_call | solution.py:1115
  178.5 8.0 %shard_map.221 = (bf16[512,768]{1,0:T(8,128)(2,1)}, bf16[512,768]{1,0:T(8,128)(2,1)}, f32[768]{0:T(1024)}, f32[576,768]{1,0:T(8,128)}, f32[576,768]{1,0:T(8,128)...) custom-call(bf16[512,768]{1,0:T(8,128)(2,1)} %get-tuple-element.29.o, ...), custom_call_target="tpu_custom_call" | custom-call | tf_op jit(solution)/shard_map/pallas_call | solution.py:1137

commit v5 on v4

--- a/solution.py
+++ b/solution.py
@@ -19,49 +19,43 @@
 MESH = pl.DeviceIdType.MESH
 
 AFTER = {
-    "norm": (("agp", 1), ("agp", 0), ("agp", 2), ("agp", 3), ("zw", 0, 1), ("zw", 0, 2), ("ag2", 0),),
-    "A0p0": (("ag1", 1), ("zw", 0, 3), ("zs", 1),),
-    "A0p2": (("ag3", 0),),
-    "A0p3": (("ag2", 1),),
-    "A0s": (("zw", 1, 1),),
-    "gate": (("zw", 1, 2), ("ag1", 2),),
-    "A1p0": (("ag1", 3),),
-    "A1p1": (("zw", 1, 3), ("ag2", 2),),
-    "A1p3": (("ag3", 1),),
-    "A2q": (("ag1", 4),),
-    "A2p0": (("ag2", 3),),
-    "A2p1": (("ag3", 2), ("ag1", 5),),
-    "A2s": (("ag2", 4),),
+    "norm": (("agp", 0),),
+    "A0q": (("agp", 1),),
+    "A0p1": (("agp", 2),),
+    "A0p2": (("agp", 3), ("zw", 0, 1), ("zw", 0, 2), ("ag2", 0), ("ag1", 1), ("zw", 0, 3),),
+    "gate": (("zs", 1), ("ag2", 1), ("ag3", 0),),
+    "A1p0": (("zw", 1, 1),),
+    "A1p1": (("ag1", 2), ("ag3", 1), ("zw", 1, 2), ("ag1", 3), ("ag2", 2),),
+    "A1p3": (("zw", 1, 3),),
+    "A2p2": (("ag1", 4),),
+    "A2p3": (("ag2", 3),),
+    "A2s": (("ag3", 2), ("ag1", 5), ("ag2", 4),),
     "F0a": (("ag3", 3),),
-    "F0b": (("ag2", 5),),
-    "F1a": (("rs0", 0),),
+    "F0c": (("ag2", 5), ("rs0", 0),),
     "F1b": (("ag3", 4),),
     "F1c": (("rs0", 1), ("rs1", 0),),
     "F2a": (("rs1", 1), ("ag3", 5),),
     "F2c": (("rs0", 2),),
-    "F3a": (("rs2", 0),),
-    "F3b": (("rs1", 2),),
+    "F3a": (("rs2", 0), ("rs1", 2),),
     "F3c": (("rs0", 3), ("rs2", 1),),
     "mid2": (("rs1", 3),),
     "outmm": (("rs0", 4),),
-    "B0o": (("rs3", 1), ("rs2", 2),),
-    "B0p0": (("rs3", 0),),
-    "B0p1": (("rs1", 4), ("zfa", 0, 2),),
-    "B0g": (("rs0", 5),),
-    "B1o": (("rs2", 3), ("g", 0), ("rs1", 5),),
-    "B1p2": (("zfa", 0, 3), ("g", 1),),
-    "B1g": (("rs0", 6), ("rs2", 4), ("rs3", 2),),
-    "B2o": (("rs2", 5), ("rs1", 6),),
-    "B2p0": (("g", 2),),
-    "B2p1": (("rs3", 3),),
-    "B2g": (("rs0", 7), ("rs3", 5), ("rs1", "z0"),),
+    "B0o": (("rs2", 2),),
+    "B0p1": (("rs1", 4), ("g", 0),),
+    "B0p2": (("zfa", 0, 2),),
+    "B0g": (("g", 1), ("rs0", 5), ("rs2", 3),),
+    "B1o": (("rs3", 0),),
+    "B1p0": (("rs3", 1), ("rs1", 5), ("rs3", 2),),
+    "B1p1": (("zfa", 0, 3),),
+    "B1g": (("rs0", 6), ("rs2", 4),),
+    "B1h": (("rs3", 3), ("rs1", 6), ("rs2", 5), ("g", 2),),
+    "B2p1": (("zza", 0, 2),),
+    "B2g": (("rs0", 7), ("rs1", "z0"), ("rs3", 4),),
     "B2h": (("rs1", 7),),
-    "B3o": (("rs2", 6), ("zza", 0, 3),),
-    "B3p1": (("rs3", 4), ("rs2", "z0"),),
-    "B3p2": (("zza", 0, 2),),
-    "B3g": (("rs0", 8), ("g", 3), ("rs2", 7), ("zza", 2, 3), ("rs3", 6), ("rs1", 8), ("rs3", "z0"), ("zza", 1, 2),),
-    "B3h": (("fin0", 0), ("g", 4),),
-    "tail": (("v", 0), ("rs2", 8), ("zza", 2, 2), ("rs3", 7), ("g", 5), ("v", 1), ("fin1", 0), ("rs3", 8), ("zza", 1, 3), ("fin0", 2), ("g", 6), ("v", 2), ("fin0", 1), ("fin1", 2), ("g", 7), ("fin1", 1), ("v", 3), ("fin2", 0), ("fin2", 2), ("fin2", 1), ("fin3", 0), ("v", 4), ("fin3", 2), ("g", 8), ("fin3", 1),),
+    "B3o": (("zza", 0, 3),),
+    "B3p0": (("g", 3), ("rs3", 5), ("rs2", 6), ("rs2", "z0"),),
+    "B3g": (("rs0", 8), ("rs2", 7), ("zza", 1, 3), ("g", 4), ("rs3", 6), ("rs1", 8), ("zza", 2, 3), ("rs3", "z0"), ("fin0", 0),),
+    "tail": (("rs3", 7), ("zza", 1, 2), ("v", 0), ("g", 5), ("rs2", 8), ("zza", 2, 2), ("v", 1), ("fin1", 0), ("rs3", 8), ("fin0", 2), ("v", 2), ("g", 6), ("fin0", 1), ("fin1", 2), ("v", 3), ("g", 7), ("fin1", 1), ("fin2", 0), ("fin2", 2), ("fin2", 1), ("v", 4), ("fin3", 0), ("g", 8), ("fin3", 2), ("fin3", 1),),
 }
 
 

time: 187 us -> 186 us (level)
  no operation moved by 1% of the time
where the time goes in v5:
time: 186 us; the launch traced here: 185 us
  Pallas kernels  185 us (99%)
    pallas_call x1, Pallas kernels, body(): pl.pallas_call(layer_kernel, out_shape=(jax.ShapeDtypeStruct((R, D), bf16...  177 us
    pallas_call x1, Pallas kernels, body(): pl.pallas_call(widen_kernel, out_shape=(jax.ShapeDtypeStruct((R, D), bf16...  8.02 us

profile of v5, /device:TPU:0, one launch (start us, length us, event | category | flops | bytes accessed | tf_op | source)
XLA Modules:
  0.0 185.3 jit_solution(16738392056023955548)
XLA Ops:
  0.6 176.6 %shard_map.220 = (bf16[512,768]{1,0:T(8,128)(2,1)}, bf16[512,768]{1,0:T(8,128)(2,1)}, bf16[2,2,768,768]{3,2,1,0:T(8,128)(2,1)}, bf16[4,2,96,768]{3,2,1,0:T(8,128)(2,1)}, f32[8,768]{1,0:T(8,128)}) custom-call(bf16[512,768]{1,0:T(8,128)(2,1)} %x_hbm.1, bf16[512,768]{1,0:T(8,128)(2,1)} %og_hbm.1, bf16[768,768]{1,0:T(8,128)(2,1)} %gate_hbm.1, ...), custom_call_target="tpu_custom_call" | custom-call | tf_op jit(solution)/shard_map/pallas_call | solution.py:1109
  177.3 8.0 %shard_map.221 = (bf16[512,768]{1,0:T(8,128)(2,1)}, bf16[512,768]{1,0:T(8,128)(2,1)}, f32[768]{0:T(1024)}, f32[576,768]{1,0:T(8,128)}, f32[576,768]{1,0:T(8,128)...) custom-call(bf16[512,768]{1,0:T(8,128)(2,1)} %get-tuple-element.29.o, ...), custom_call_target="tpu_custom_call" | custom-call | tf_op jit(solution)/shard_map/pallas_call | solution.py:1131

commit v6 on v5

--- a/solution.py
+++ b/solution.py
@@ -562,78 +562,73 @@
         ys, yo = blk(YH * y, YH, 128), blk(YH * (1 - y), YH, 128)
         src, dst, dev = {
             0: lambda: (gg.at[:, 1 - c], gcr, dev_c),
-            1: lambda: (gg.at[:, c, xo, :], gxr, dev_x),
-            2: lambda: (gg.at[:, c, xs, yo], gyr, dev_y),
-            3: lambda: (gout.at[:, c, xs, ys], gout.at[:, c, xs, ys], dev_y),
-            4: lambda: (gout.at[:, c, xs, :], gout.at[:, c, xs, :], dev_x),
+            1: lambda: (gg.at[z, c, xo, :], gxr, dev_x),
+            2: lambda: (gg.at[z, c, xs, yo], gyr, dev_y),
+            3: lambda: (gg.at[z, c, xs, ys], gout.at[z, c, xs, ys], dev_y),
+            4: lambda: (gout.at[z, c, xs, :], gout.at[z, c, xs, :], dev_x),
             5: lambda: (gout.at[:, c], gout.at[:, c], dev_c),
         }[i]()
         return remote(src, dst, g_s.at[i], g_r.at[i], dev)
 
     def g_z(slot, rslot):
-        src = gg.at[zof(slot), c, blk(GX * x, GX, 16), blk(YH * y, YH, 128)]
-        return remote(src, gzr.at[rslot - 1], gz_s.at[slot], gz_r.at[rslot], (dp, zof(slot)))
+        return remote(
+            gg.at[zof(slot), c], gzr.at[rslot - 1], gz_s.at[slot], gz_r.at[rslot], (dp, zof(slot))
+        )
 
     def g_za(slot, rslot):
-        src = gg.at[z, c, blk(GX * x, GX, 16), blk(YH * y, YH, 128)]
-        dst = gout.at[z, c, blk(GX * x, GX, 16), blk(YH * y, YH, 128)]
-        return remote(src, dst, ga_s.at[slot], ga_r.at[rslot], (dp, zof(slot)))
+        return remote(gout.at[z, c], gout.at[z, c], ga_s.at[slot], ga_r.at[rslot], (dp, zof(slot)))
 
     def g_local():
-        src = gg.at[z, c, blk(GX * x, GX, 16), blk(YH * y, YH, 128)]
-        dst = gout.at[z, c, blk(GX * x, GX, 16), blk(YH * y, YH, 128)]
-        return pltpu.make_async_copy(src, dst, gl.at[0])
+        xs, ys = blk(GX * x, GX, 16), blk(YH * y, YH, 128)
+        return pltpu.make_async_copy(gg.at[z, c, xs, ys], gout.at[z, c, xs, ys], gl.at[0])
 
     def g_step(i):
-        xs, ys = blk(GX * x, GX, 16), blk(YH * y, YH, 128)
         if i == 0:
             g_copy(0).start()
         if i == 1:
             g_copy(0).wait_recv()
             for q in range(4):
                 add_rows(gg, (q, c), 0, 2 * GX, 0, D, gcr, (q,))
-            g_copy(1).start()
+            for slot in range(1, 4):
+                g_z(slot, seen_as(slot)).start()
             g_copy(0).wait_send()
         if i == 2:
+            for slot in range(1, 4):
+                g_z(slot, slot).wait_recv()
+            t = gg[z, c].astype(f32)
+            for slot in range(3):
+                t = t + gzr[slot].astype(f32)
+            gg[z, c] = t.astype(bf16)
+            g_copy(1).start()
+            for slot in range(1, 4):
+                g_z(slot, slot).wait_send()
+        if i == 3:
             g_copy(1).wait_recv()
-            for q in range(4):
-                add_rows(gg, (q, c), GX * x, GX, 0, D, gxr, (q,))
+            add_rows(gg, (z, c), GX * x, GX, 0, D, gxr, ())
             g_copy(2).start()
             g_copy(1).wait_send()
-        if i == 3:
+        if i == 4:
             g_copy(2).wait_recv()
-            for q in range(4):
-                add_rows(gg, (q, c), GX * x, GX, YH * y, YH, gyr, (q,))
-            for slot in range(1, 4):
-                g_z(slot, seen_as(slot)).start()
+            add_rows(gg, (z, c), GX * x, GX, YH * y, YH, gyr, ())
+            g_local().start()
+            g_copy(3).start()
             g_copy(2).wait_send()
-        if i == 4:
-            for slot in range(1, 4):
-                g_z(slot, slot).wait_recv()
-            t = gg[z, c, xs, ys].astype(f32)
-            for slot in range(3):
-                t = t + gzr[slot].astype(f32)
-            gg[z, c, xs, ys] = t.astype(bf16)
-            g_local().start()
+        if i == 5:
+            g_copy(3).wait_recv()
+            g_local().wait()
+            g_copy(4).start()
+            g_copy(3).wait_send()
+        if i == 6:
+            g_copy(4).wait_recv()
             for slot in range(1, 4):
                 g_za(slot, seen_as(slot)).start()
-            for slot in range(1, 4):
-                g_z(slot, slot).wait_send()
-        if i == 5:
+            g_copy(4).wait_send()
+        if i == 7:
             for slot in range(1, 4):
                 g_za(slot, slot).wait_recv()
-            g_local().wait()
-            g_copy(3).start()
+            g_copy(5).start()
             for slot in range(1, 4):
                 g_za(slot, slot).wait_send()
-        if i == 6:
-            g_copy(3).wait_recv()
-            g_copy(4).start()
-            g_copy(3).wait_send()
-        if i == 7:
-            g_copy(4).wait_recv()
-            g_copy(5).start()
-            g_copy(4).wait_send()
         if i == 8:
             g_copy(5).wait_recv()
             g_copy(5).wait_send()
@@ -1077,9 +1072,9 @@
         pltpu.VMEM((ZF // 2, YH), bf16),
         pltpu.VMEM((4, 2, 2 * GX, D), bf16),
         pltpu.VMEM((4, 2 * GX, D), bf16),
-        pltpu.VMEM((4, GX, D), bf16),
-        pltpu.VMEM((4, GX, YH), bf16),
-        pltpu.VMEM((3, GX, YH), bf16),
+        pltpu.VMEM((GX, D), bf16),
+        pltpu.VMEM((GX, YH), bf16),
+        pltpu.VMEM((3, 2 * GX, D), bf16),
         pltpu.VMEM((3, 8, D), f32),
         pltpu.VMEM((3, 8, D), f32),
         pltpu.VMEM((4, 8, D), f32),

time: 186 us -> 183 us (0.984)
  Pallas kernels: 185 us -> 182 us
    pallas_call x1, Pallas kernels: 177 us -> 174 us  [body(): pl.pallas_call(layer_kernel, out_shape=(jax.ShapeDtypeStruct((R, D), bf16...]
where the time goes in v6:
time: 183 us; the launch traced here: 182 us
  Pallas kernels  182 us (99%)
    pallas_call x1, Pallas kernels, body(): pl.pallas_call(layer_kernel, out_shape=(jax.ShapeDtypeStruct((R, D), bf16...  174 us
    pallas_call x1, Pallas kernels, body(): pl.pallas_call(widen_kernel, out_shape=(jax.ShapeDtypeStruct((R, D), bf16...  8.02 us

profile of v6, /device:TPU:0, one launch (start us, length us, event | category | flops | bytes accessed | tf_op | source)
XLA Modules:
  0.0 182.5 jit_solution(13442543476399167433)
XLA Ops:
  0.6 173.8 %shard_map.220 = (bf16[512,768]{1,0:T(8,128)(2,1)}, bf16[512,768]{1,0:T(8,128)(2,1)}, bf16[2,2,768,768]{3,2,1,0:T(8,128)(2,1)}, bf16[4,2,96,768]{3,2,1,0:T(8,128)(2,1)}, f32[8,768]{1,0:T(8,128)}) custom-call(bf16[512,768]{1,0:T(8,128)(2,1)} %x_hbm.1, bf16[512,768]{1,0:T(8,128)(2,1)} %og_hbm.1, bf16[768,768]{1,0:T(8,128)(2,1)} %gate_hbm.1, ...), custom_call_target="tpu_custom_call" | custom-call | tf_op jit(solution)/shard_map/pallas_call | solution.py:1104
  174.4 8.0 %shard_map.221 = (bf16[512,768]{1,0:T(8,128)(2,1)}, bf16[512,768]{1,0:T(8,128)(2,1)}, f32[768]{0:T(1024)}, f32[576,768]{1,0:T(8,128)}, f32[576,768]{1,0:T(8,128)...) custom-call(bf16[512,768]{1,0:T(8,128)(2,1)} %get-tuple-element.29.o, ...), custom_call_target="tpu_custom_call" | custom-call | tf_op jit(solution)/shard_map/pallas_call | solution.py:1126
